TPU v7x, 512 devices: a whole 4x8x8 slice. The times are simulated.
512 devices in a mesh: row: 16 (over y, core), col: 8 (over z), depth: 4 (over x).
Axes of the slice: x: 4, y: 8, z: 8, core: 2. Of those that a mesh axis runs over, the one named last changes fastest.
Arguments:
- density: float32 [512, 5, 128, 128], P(('row', 'depth'), None, 'col'), may hold values from -0.6 to 0.6
- pattern: int32 [512, 5], P(('row', 'depth')), may hold values 0 or 1
Outputs:
- purified: float32 [512, 5, 128, 128], P(('row', 'depth'), None, 'col')
All inputs are finite; a program needn't handle non-finite values. No bound on the sum of `pattern` on one device may be relied on, other than what follows from the above.
Results may differ from a plain program's by a relative error of at most 0.0001.
Values sent between devices are 32-bit elements; how exact they have to be, the bound alone decides.
No kernel may reach another device: no remote copies, remote signals or barrier semaphores. Data moves between devices by JAX's collectives and lax.ppermute only.
A program may use at most 64 MiB of HBM per device.

v0:
```python
import jax
import jax.numpy as jnp
from jax import lax
from jax.sharding import PartitionSpec as P

HALF = 2
WIDE = 5


def with_halo(cells, sides, width):
    for axis, dim in sides:
        count = lax.axis_size(axis)
        head = lax.slice_in_dim(cells, 0, width, axis=dim)
        tail = lax.slice_in_dim(cells, cells.shape[dim] - width, cells.shape[dim], axis=dim)
        cells = jnp.concatenate(
            [
                lax.ppermute(tail, axis, [(i, (i + 1) % count) for i in range(count)]),
                cells,
                lax.ppermute(head, axis, [((i + 1) % count, i) for i in range(count)]),
            ],
            axis=dim,
        )
    return cells


def banded_local(left_tiles, extended, pattern):
    rows_here = left_tiles.shape[0]
    summed = jnp.zeros(left_tiles.shape, jnp.float32)
    for source in range(WIDE):
        first_slot = max(0, source - HALF)
        last_slot = min(WIDE, source + HALF + 1)
        partner = extended[
            source : source + rows_here, first_slot - source + HALF : last_slot - source + HALF
        ]
        contrib = jnp.einsum(
            "iab,itbc->itac", left_tiles[:, source], partner, precision=lax.Precision.HIGHEST
        )
        summed = summed.at[:, first_slot:last_slot].add(contrib)
    return summed * pattern[:, :, None, None].astype(jnp.float32)


def shards(density, pattern):
    masked = density * pattern[:, :, None, None].astype(jnp.float32)
    whole_tiles = lax.all_gather(masked, "col", axis=2, tiled=True)
    extended = with_halo(whole_tiles, ((("row", "depth"), 0),), HALF)
    square = banded_local(masked, extended, pattern)
    cube = banded_local(square, extended, pattern)
    return 3.0 * square - 2.0 * cube


def solution(mesh):
    in_specs = (P(("row", "depth"), None, "col", None), P(("row", "depth"), None))
    out_specs = P(("row", "depth"), None, "col", None)
    return jax.shard_map(shards, mesh=mesh, in_specs=in_specs, out_specs=out_specs, check_vma=False)
```

profile of v0, /device:TPU:1, one launch (start us, length us, event | category | flops | bytes accessed | tf_op | source)
XLA Modules:
  0.0 108.2 jit_solution(13460640927756689920)
XLA Ops:
  6.5 0.0 all-gather.2.cloned.1.call-start
  6.5 0.7 convert_element_type.6
  7.2 0.1 copy.3
  7.3 1.8 %copy_multiply_fusion = f32[8,5,16,128]{3,2,0,1:T(8,128)} fusion(f32[8,5,16,128]{3,2,1,0:T(8,128)} %param.26, f32[8,5]{0,1:T(8,128)S(1)} %copy.3), kind=kLoop, calls=%fused_computation.18 | loop fusion | flops 81920 | bytes 655520 | tf_op jit(solution)/shard_map/mul | solution.py:43
  9.1 0.0 all-gather.2.cloned.1.call-update
  9.1 48.3 %all-gather.2.cloned.1.call-done = f32[8,5,128,128]{3,2,0,1:T(8,128)} async-done(((f32[8,5,16,128]{3,2,0,1:T(8,128)}), f32[8,5,128,128]{3,2,0,1:T(8,128)}) %all-gather.2.cloned.1.call-update) | async-done | bytes 2621456 | tf_op jit(solution)/shard_map/all_gather | solution.py:44
  57.5 0.0 copy-start
  57.5 1.5 %fusion.10 = (f32[2,5,128,128]{3,2,0,1:T(8,128)S(1)}, f32[2,5,128,128]{3,2,0,1:T(8,128)S(1)}) fusion(f32[8,5,128,128]{3,2,0,1:T(8,128)} %all-gather.2.cloned.1.call-done), kind=kLoop, calls=%fused_computation.41 | loop fusion | bytes 2621440 | tf_op jit(solution)/shard_map/slice | solution.py:13
  59.0 3.1 %collective-permute-start = (f32[2,5,128,128]{3,2,0,1:T(8,128)S(1)}, f32[2,5,128,128]{3,2,0,1:T(8,128)S(1)}, u32[]{:S(2)}, u32[]{:S(2)}) collective-permute-start(f32[2,5,128,128]{3,2,0,1:T(8,128)S(1)} %get-tuple-element.142), channel_id=1, source_target_pairs={{0,1},{1,2},{2,3},{3,32},{32,33},{33,34},{34,35},{35,64},{64,65},{... | collective-permute-start | bytes 1966088 | tf_op jit(solution)/shard_map/ppermute | solution.py:17
  62.1 6.9 %collective-permute-start.1 = (f32[2,5,128,128]{3,2,0,1:T(8,128)S(1)}, f32[2,5,128,128]{3,2,0,1:T(8,128)S(1)}, u32[]{:S(2)}, u32[]{:S(2)}) collective-permute-start(f32[2,5,128,128]{3,2,0,1:T(8,128)S(1)} %get-tuple-element.141), channel_id=1, source_target_pairs={{1,0},{2,1},{3,2},{32,3},{33,32},{34,33},{35,34},{64,35},{65,64},{... | collective-permute-start | bytes 1966088 | tf_op jit(solution)/shard_map/ppermute | solution.py:19
  69.1 13.3 %collective-permute-done = f32[2,5,128,128]{3,2,0,1:T(8,128)S(1)} collective-permute-done((f32[2,5,128,128]{3,2,0,1:T(8,128)S(1)}, f32[2,5,128,128]{3,2,0,1:T(8,128)S(1)}, u32[]{:S(2)}, u32[]{:S(2)}) %collective-permute-start) | collective-permute-done | bytes 655392 | tf_op jit(solution)/shard_map/ppermute | solution.py:17
  82.5 0.0 copy-done
  82.5 0.0 copy-start.1
  82.5 0.6 constant_dynamic-update-slice_fusion.3
  83.1 0.3 copy-done.1
  83.5 1.4 %convolution_bitcast_fusion.9 = f32[8,3,16,128]{3,2,0,1:T(8,128)S(1)} fusion(f32[10,5,128,128]{3,2,0,1:T(8,128)S(1)} %get-tuple-element.144, f32[8,5,16,128]{3,2,0,1:T(8,128)S(1)} %copy-done.1), kind=kOutput, calls=%fused_computation.17 | convolution fusion | flops 75497472 | bytes 3538944 | tf_op jit(solution)/shard_map/iab,itbc->itac/dot_general | solution.py:35
  84.9 1.9 %fusion.7 = f32[8,5,16,128]{3,2,0,1:T(8,128)S(1)} fusion(f32[8,5,16,128]{3,2,0,1:T(8,128)S(1)} %scatter-add.26, f32[10,5,128,128]{3,2,0,1:T(8,128)S(1)} %get-tuple-element.144, f32[8,5,16,128]{3,2,0,1:T(8,128)S(1)} %copy-done.1), kind=kOutput, calls=%fused_computation.13 | convolution fusion | flops 100728832 | bytes 3866624 | tf_op jit(solution)/shard_map/iab,itbc->itac/dot_general | solution.py:35
  86.8 1.7 %fusion.1 = f32[8,5,16,128]{3,2,0,1:T(8,128)S(1)} fusion(f32[8,5,16,128]{3,2,0,1:T(8,128)S(1)} %fusion.7, f32[8,5,128,128]{3,2,0,1:T(8,128)S(1)} %copy-done, f32[8,5,16,128]{3,2,0,1:T(8,128)S(1)} %copy-done.1), kind=kOutput, calls=%fused_computation.3 | convolution fusion | flops 125911040 | bytes 3342336 | tf_op jit(solution)/shard_map/iab,itbc->itac/dot_general | solution.py:35
  88.4 0.0 collective-permute-done.1
  88.5 1.9 %fusion.5 = f32[8,4,16,128]{3,2,0,1:T(8,128)S(1)} fusion(f32[10,5,128,128]{3,2,0,1:T(8,128)S(1)} %constant_dynamic-update-slice_fusion.2, f32[8,5,16,128]{3,2,0,1:T(8,128)S(1)} %fusion.1, f32[8,5,16,128]{3,2,0,1:T(8,128)S(1)} %copy-done.1), kind=kOutput, calls=%fused_computation.10 | convolution fusion | flops 100728832 | bytes 3866624 | tf_op jit(solution)/shard_map/iab,itbc->itac/dot_general | solution.py:35
  90.4 1.4 %fusion.9 = f32[8,5,16,128]{3,2,0,1:T(8,128)S(1)} fusion(f32[8,5,16,128]{3,2,0,1:T(8,128)S(1)} %constant_dynamic-update-slice_fusion.5, f32[8,4,16,128]{3,2,0,1:T(8,128)S(1)} %fusion.5, f32[10,5,128,128]{3,2,0,1:T(8,128)S(1)} %constant_dynamic-update-slice_fusion.2, f32[8,5,16,128]{3,2,0,1:T(8,128)S(1)} %copy-done.1), kind=kOutput, calls=%fused_computation.23 | convolution fusion | flops 75546624 | bytes 3735552 | tf_op jit(solution)/shard_map/iab,itbc->itac/dot_general | solution.py:35
  91.8 0.1 broadcast_multiply_fusion
  92.0 1.4 %convolution_bitcast_fusion.7 = f32[8,3,16,128]{3,2,0,1:T(8,128)S(1)} fusion(f32[10,5,128,128]{3,2,0,1:T(8,128)S(1)} %get-tuple-element.144, f32[8,5,16,128]{3,2,0,1:T(8,128)S(1)} %broadcast_multiply_fusion), kind=kOutput, calls=%fused_computation.15 | convolution fusion | flops 75497472 | bytes 3538944 | tf_op jit(solution)/shard_map/iab,itbc->itac/dot_general | solution.py:35
  93.4 1.9 %fusion.4 = f32[8,5,16,128]{3,2,0,1:T(8,128)S(1)} fusion(f32[8,5,16,128]{3,2,0,1:T(8,128)S(1)} %scatter-add.34, f32[10,5,128,128]{3,2,0,1:T(8,128)S(1)} %get-tuple-element.144, f32[8,5,16,128]{3,2,0,1:T(8,128)S(1)} %broadcast_multiply_fusion), kind=kOutput, calls=%fused_computation.8 | convolution fusion | flops 100728832 | bytes 3866624 | tf_op jit(solution)/shard_map/iab,itbc->itac/dot_general | solution.py:35
  95.3 1.8 %fusion = f32[8,5,16,128]{3,2,0,1:T(8,128)S(1)} fusion(f32[8,5,16,128]{3,2,0,1:T(8,128)S(1)} %fusion.4, f32[8,5,128,128]{3,2,0,1:T(8,128)S(1)} %copy-done, f32[8,5,16,128]{3,2,0,1:T(8,128)S(1)} %broadcast_multiply_fusion), kind=kOutput, calls=%fused_computation.1 | convolution fusion | flops 125911040 | bytes 3342336 | tf_op jit(solution)/shard_map/iab,itbc->itac/dot_general | solution.py:35
  97.1 1.9 %fusion.2 = f32[8,4,16,128]{3,2,0,1:T(8,128)S(1)} fusion(f32[10,5,128,128]{3,2,0,1:T(8,128)S(1)} %constant_dynamic-update-slice_fusion.2, f32[8,5,16,128]{3,2,0,1:T(8,128)S(1)} %fusion, f32[8,5,16,128]{3,2,0,1:T(8,128)S(1)} %broadcast_multiply_fusion), kind=kOutput, calls=%fused_computation.5 | convolution fusion | flops 100728832 | bytes 3866624 | tf_op jit(solution)/shard_map/iab,itbc->itac/dot_general | solution.py:35
  99.0 1.4 %fusion.8 = f32[8,5,16,128]{3,2,0,1:T(8,128)S(1)} fusion(f32[8,5,16,128]{3,2,0,1:T(8,128)S(1)} %constant_dynamic-update-slice_fusion.4, f32[8,4,16,128]{3,2,0,1:T(8,128)S(1)} %fusion.2, f32[10,5,128,128]{3,2,0,1:T(8,128)S(1)} %constant_dynamic-update-slice_fusion.2, f32[8,5,16,128]{3,2,0,1:T(8,128)S(1)} %broadcast_multiply_fusion), kind=kOutput, calls=%fused_computation.21 | convolution fusion | flops 75546624 | bytes 3735552 | tf_op jit(solution)/shard_map/iab,itbc->itac/dot_general | solution.py:35
  100.5 0.1 multiply_subtract_fusion
  100.6 0.7 copy.25
  (6 shorter events, 0.2 us)
Async XLA Ops:
  6.5 50.9 %all-gather.2.cloned.1.call-start = ((), (), s32[]{:S(2)}) async-start(), calls=%async_computation | async-start | bytes 2949120 | tf_op jit(solution)/shard_map/all_gather | solution.py:44
  57.5 25.0 %copy-start = (f32[8,5,128,128]{3,2,0,1:T(8,128)S(1)}, f32[8,5,128,128]{3,2,0,1:T(8,128)}, u32[]{:S(2)}) copy-start(f32[8,5,128,128]{3,2,0,1:T(8,128)} %all-gather.2.cloned.1.call-done) | copy-start | bytes 7864324
  59.0 23.4 %collective-permute-start = (f32[2,5,128,128]{3,2,0,1:T(8,128)S(1)}, f32[2,5,128,128]{3,2,0,1:T(8,128)S(1)}, u32[]{:S(2)}, u32[]{:S(2)}) collective-permute-start(f32[2,5,128,128]{3,2,0,1:T(8,128)S(1)} %get-tuple-element.142), channel_id=1, source_target_pairs={{0,1},{1,2},{2,3},{3,32},{32,33},{33,34},{34,35},{35,64},{64,65},{... | collective-permute-start | bytes 1966088 | tf_op jit(solution)/shard_map/ppermute | solution.py:17
  62.1 26.3 %collective-permute-start.1 = (f32[2,5,128,128]{3,2,0,1:T(8,128)S(1)}, f32[2,5,128,128]{3,2,0,1:T(8,128)S(1)}, u32[]{:S(2)}, u32[]{:S(2)}) collective-permute-start(f32[2,5,128,128]{3,2,0,1:T(8,128)S(1)} %get-tuple-element.141), channel_id=1, source_target_pairs={{1,0},{2,1},{3,2},{32,3},{33,32},{34,33},{35,34},{64,35},{65,64},{... | collective-permute-start | bytes 1966088 | tf_op jit(solution)/shard_map/ppermute | solution.py:19
  82.5 1.0 copy-start.1
Sparse Core Ops, SparseCore 0:
  9.4 47.9 all-gather.1
where the time goes:
time: 108 us
  waiting for transfers between devices  61.7 us (57%)
  matrix products  16.7 us (15%)
  between operations  13.5 us (12%)
  starting transfers between devices  10 us (9%)
  local copies, waits for them, and re-layouts  3.51 us (3%)
  other arithmetic  2.73 us (3%)
    all_gather x1, waiting for transfers between devices, shards(): whole_tiles = lax.all_gather(masked, 'col', axis=2, tiled=True)  48.3 us
    dot_general x10, matrix products, banded_local(): jnp.einsum('iab,itbc->itac', left_tiles[:, source], partner, precision=la...  16.7 us
    ppermute x1, waiting for transfers between devices, with_halo(): lax.ppermute(tail, axis, [(i, (i + 1) % count) for i in range(count)])  13.3 us
    ppermute x1, starting transfers between devices, with_halo(): lax.ppermute(head, axis, [((i + 1) % count, i) for i in range(count)])  6.94 us
    ppermute x1, starting transfers between devices, with_halo(): lax.ppermute(tail, axis, [(i, (i + 1) % count) for i in range(count)])  3.1 us
  transfers between devices with their start and end apart: 3, of which 2 were waited for; matrix products, arithmetic and copies ran while one was open for 5% of the time, Pallas kernels for 0%

commit v1 on v0

v1 whole, which is shorter than its diff:
```python
import jax
import jax.numpy as jnp
from jax import lax
from jax.experimental import pallas as pl
from jax.experimental.pallas import tpu as pltpu
from jax.sharding import PartitionSpec as P

HALF = 2
WIDE = 5
AXES = ("row", "col", "depth")


def ring_pairs(sizes, shift):
    rows, cols, depths = sizes
    total = rows * cols * depths

    def place(i):
        chunk, col = divmod(i % total, cols)
        row, depth = divmod(chunk, depths)
        return (row * cols + col) * depths + depth

    return [(place(i + shift), place(i)) for i in range(total)]


def halves(value):
    high = value.astype(jnp.bfloat16)
    return high, (value - high.astype(jnp.float32)).astype(jnp.bfloat16)


def dot(left, right):
    return jnp.dot(left, right, preferred_element_type=jnp.float32)


def band_kernel(pattern_ref, own_ref, m2_ref, m1_ref, p1_ref, p2_ref, out_ref):
    stored = (m2_ref, m1_ref, own_ref, p1_ref, p2_ref)
    first = (2, 1, 0, 0, 0)
    right = {}
    for u in range(WIDE):
        for s in range(stored[u].shape[0]):
            right[u, s + first[u]] = halves(stored[u][s])
    keep = [pattern_ref[t].astype(jnp.float32) for t in range(WIDE)]

    def product(left):
        result = []
        for t in range(WIDE):
            summed = None
            for u in range(max(0, t - HALF), min(WIDE, t + HALF + 1)):
                high, low = left[u]
                other_high, other_low = right[u, t - u + HALF]
                term = dot(high, other_high) + dot(high, other_low) + dot(low, other_high)
                summed = term if summed is None else summed + term
            result.append(summed * keep[t])
        return result

    square = product([right[HALF, s] for s in range(WIDE)])
    cube = product([halves(block) for block in square])
    for t in range(WIDE):
        out_ref[:, t] = (3.0 * square[t] - 2.0 * cube[t]).reshape(out_ref.shape[0], -1, out_ref.shape[3])


def shards(density, pattern):
    sizes = tuple(lax.axis_size(a) for a in AXES)
    cols, wide, rows, width = density.shape
    keep = lax.dynamic_index_in_dim(pattern, lax.axis_index("col"), 0, keepdims=False)
    parts = lax.all_to_all(density, "col", 0, 0, tiled=True)
    own = jnp.swapaxes(parts, 0, 1) * keep.astype(jnp.float32)[:, None, None, None]
    own = own.reshape(wide, cols * rows, width)
    p1 = lax.ppermute(own[:4], AXES, ring_pairs(sizes, 1))
    m1 = lax.ppermute(own[1:], AXES, ring_pairs(sizes, -1))
    p2 = lax.ppermute(own[:3], AXES, ring_pairs(sizes, 2))
    m2 = lax.ppermute(own[2:], AXES, ring_pairs(sizes, -2))
    vmem = pl.BlockSpec(memory_space=pltpu.VMEM)
    result = pl.pallas_call(
        band_kernel,
        out_shape=jax.ShapeDtypeStruct(density.shape, jnp.float32),
        in_specs=[pl.BlockSpec(memory_space=pltpu.SMEM)] + [vmem] * 5,
        out_specs=vmem,
        compiler_params=pltpu.CompilerParams(vmem_limit_bytes=32 * 1024 * 1024),
    )(keep, own, m2, m1, p1, p2)
    return lax.all_to_all(result, "col", 0, 0, tiled=True)


def solution(mesh):
    in_specs = (P(("row", "depth"), None, "col", None), P(("row", "depth"), None))
    out_specs = P(("row", "depth"), None, "col", None)
    return jax.shard_map(shards, mesh=mesh, in_specs=in_specs, out_specs=out_specs, check_vma=False)
```

time: 108 us -> 70.4 us (0.65)
  the two profiles are of different devices: /device:TPU:1 before, /device:TPU:31 now
where the time goes in v1:
time: 70.4 us; the launch traced here: 70 us
  starting transfers between devices  25.7 us (37%)
  blocking collectives  24 us (34%)
  waiting for transfers between devices  16.9 us (24%)
  Pallas kernels  1.69 us (2%)
  local copies, waits for them, and re-layouts  0.88 us (1%)
  other arithmetic  0.78 us (1%)
    all_to_all x1, blocking collectives, shards(): return lax.all_to_all(result, 'col', 0, 0, tiled=True)  24 us
    all_to_all x1, waiting for transfers between devices, shards(): parts = lax.all_to_all(density, 'col', 0, 0, tiled=True)  11.2 us
    all_to_all x1, starting transfers between devices, shards(): parts = lax.all_to_all(density, 'col', 0, 0, tiled=True)  10 us
    ppermute x1, starting transfers between devices, shards(): p2 = lax.ppermute(own[:3], AXES, ring_pairs(sizes, 2))  6.37 us
    ppermute x1, starting transfers between devices, shards(): p1 = lax.ppermute(own[:4], AXES, ring_pairs(sizes, 1))  5.47 us
    ppermute x1, waiting for transfers between devices, shards(): m2 = lax.ppermute(own[2:], AXES, ring_pairs(sizes, -2))  3.59 us
    ppermute x1, waiting for transfers between devices, shards(): p2 = lax.ppermute(own[:3], AXES, ring_pairs(sizes, 2))  2.04 us
    ppermute x1, starting transfers between devices, shards(): m1 = lax.ppermute(own[1:], AXES, ring_pairs(sizes, -1))  1.92 us
  transfers between devices with their start and end apart: 5, of which 3 were waited for; matrix products, arithmetic and copies ran while one was open for 1% of the time, Pallas kernels for 0%

profile of v1, /device:TPU:31, one launch (start us, length us, event | category | flops | bytes accessed | tf_op | source)
XLA Modules:
  0.0 70.0 jit_solution(12042500001472699981)
XLA Ops:
  0.0 10.0 %all-to-all-start = ((f32[8,5,16,128]{3,2,1,0:T(8,128)}), f32[8,5,16,128]{3,2,1,0:T(8,128)S(1)}, u32[]{:S(2)}, u32[]{:S(2)}) async-start(f32[8,5,16,128]{3,2,1,0:T(8,128)} %param.2), calls=%async_computation | async-start | bytes 655360 | tf_op jit(solution)/shard_map/all_to_all | solution.py:65
  10.0 0.7 fusion
  10.7 11.2 %all-to-all-done = f32[8,5,16,128]{3,2,1,0:T(8,128)S(1)} async-done(((f32[8,5,16,128]{3,2,1,0:T(8,128)}), f32[8,5,16,128]{3,2,1,0:T(8,128)S(1)}, u32[]{:S(2)}, u32[]{:S(2)}) %all-to-all-start) | async-done | bytes 327712 | tf_op jit(solution)/shard_map/all_to_all | solution.py:65
  22.0 0.1 multiply_bitcast_fusion
  22.2 1.9 %collective-permute-start.1 = (f32[4,128,128]{2,1,0:T(8,128)S(1)}, f32[4,128,128]{2,1,0:T(8,128)S(1)}, u32[]{:S(2)}, u32[]{:S(2)}) collective-permute-start(f32[4,128,128]{2,1,0:T(8,128)S(1)} %bitcast.12), channel_id=1, source_target_pairs={{511,0},{0,4},{4,8},{8,12},{12,16},{16,20},{20,24},{24,28},{28,1},... | collective-permute-start | bytes 786440 | tf_op jit(solution)/shard_map/ppermute | solution.py:69
  24.1 5.5 %collective-permute-start.2 = (f32[4,128,128]{2,1,0:T(8,128)S(1)}, f32[4,128,128]{2,1,0:T(8,128)S(1)}, u32[]{:S(2)}, u32[]{:S(2)}) collective-permute-start(f32[4,128,128]{2,1,0:T(8,128)S(1)} %bitcast.11), channel_id=1, source_target_pairs={{4,0},{8,4},{12,8},{16,12},{20,16},{24,20},{28,24},{1,28},{5,1},{9... | collective-permute-start | bytes 786440 | tf_op jit(solution)/shard_map/ppermute | solution.py:68
  29.6 1.9 %collective-permute-start = (f32[3,128,128]{2,1,0:T(8,128)S(1)}, f32[3,128,128]{2,1,0:T(8,128)S(1)}, u32[]{:S(2)}, u32[]{:S(2)}) collective-permute-start(f32[3,128,128]{2,1,0:T(8,128)S(1)} %bitcast.14), channel_id=1, source_target_pairs={{507,0},{511,4},{0,8},{4,12},{8,16},{12,20},{16,24},{20,28},{24,1}... | collective-permute-start | bytes 589832 | tf_op jit(solution)/shard_map/ppermute | solution.py:71
  31.6 6.4 %collective-permute-start.3 = (f32[3,128,128]{2,1,0:T(8,128)S(1)}, f32[3,128,128]{2,1,0:T(8,128)S(1)}, u32[]{:S(2)}, u32[]{:S(2)}) collective-permute-start(f32[3,128,128]{2,1,0:T(8,128)S(1)} %bitcast.13), channel_id=1, source_target_pairs={{8,0},{12,4},{16,8},{20,12},{24,16},{28,20},{1,24},{5,28},{9,1},{1... | collective-permute-start | bytes 589832 | tf_op jit(solution)/shard_map/ppermute | solution.py:70
  38.0 3.6 %collective-permute-done.m2_ref = f32[3,128,128]{2,1,0:T(8,128)S(1)} collective-permute-done((f32[3,128,128]{2,1,0:T(8,128)S(1)}, f32[3,128,128]{2,1,0:T(8,128)S(1)}, u32[]{:S(2)}, u32[]{:S(2)}) %collective-permute-start) | collective-permute-done | bytes 196640 | tf_op jit(solution)/shard_map/ppermute | solution.py:71
  41.6 2.0 %collective-permute-done.3.p2_ref = f32[3,128,128]{2,1,0:T(8,128)S(1)} collective-permute-done((f32[3,128,128]{2,1,0:T(8,128)S(1)}, f32[3,128,128]{2,1,0:T(8,128)S(1)}, u32[]{:S(2)}, u32[]{:S(2)}) %collective-permute-start.3) | collective-permute-done | bytes 196640 | tf_op jit(solution)/shard_map/ppermute | solution.py:70
  43.6 0.0 collective-permute-done.1.m1_ref
  43.6 0.0 collective-permute-done.2.p1_ref
  43.6 1.7 %shard_map.28 = f32[8,5,16,128]{3,2,1,0:T(8,128)S(1)} custom-call(s32[5]{0:T(128)S(1)} %get-tuple-element.6.pattern_ref, f32[5,128,128]{2,1,0:T(8,128)S(1)} %bitcast.10, f32[3,128,128]{2,1,0:T(8,128)S(1)} %collective-permute-done.m2_ref, f32[4,128,128]{2,1,0:T(8,128)S(1)} %collective-permute-done.1.m1_ref, f32[4,128,128]{2,1,0:T(8,128)S(1)} %collective-permute-done.2.p1_ref, ...), custom_call_target="tpu_custom_call" | custom-call | tf_op jit(solution)/shard_map/pallas_call | solution.py:73
  45.3 24.0 %all_to_all.10 = f32[8,5,16,128]{3,2,1,0:T(8,128)S(1)} all-to-all(f32[8,5,16,128]{3,2,1,0:T(8,128)S(1)} %shard_map.28), channel_id=1, replica_groups=mesh['row'=16,'col'=8,'depth'=4] {'col'}, dimensions={0} | all-to-all | bytes 655360 | tf_op jit(solution)/shard_map/all_to_all | solution.py:80
  69.3 0.7 %copy.9 = f32[8,5,16,128]{3,2,1,0:T(8,128)} copy(f32[8,5,16,128]{3,2,1,0:T(8,128)S(1)} %all_to_all.10) | data formatting | bytes 655360
  (7 shorter events, 0.2 us)
Async XLA Ops:
  0.0 22.0 %all-to-all-start = ((f32[8,5,16,128]{3,2,1,0:T(8,128)}), f32[8,5,16,128]{3,2,1,0:T(8,128)S(1)}, u32[]{:S(2)}, u32[]{:S(2)}) async-start(f32[8,5,16,128]{3,2,1,0:T(8,128)} %param.2), calls=%async_computation | async-start | bytes 655360 | tf_op jit(solution)/shard_map/all_to_all | solution.py:65
  22.2 21.5 %collective-permute-start.1 = (f32[4,128,128]{2,1,0:T(8,128)S(1)}, f32[4,128,128]{2,1,0:T(8,128)S(1)}, u32[]{:S(2)}, u32[]{:S(2)}) collective-permute-start(f32[4,128,128]{2,1,0:T(8,128)S(1)} %bitcast.12), channel_id=1, source_target_pairs={{511,0},{0,4},{4,8},{8,12},{12,16},{16,20},{20,24},{24,28},{28,1},... | collective-permute-start | bytes 786440 | tf_op jit(solution)/shard_map/ppermute | solution.py:69
  24.1 19.5 %collective-permute-start.2 = (f32[4,128,128]{2,1,0:T(8,128)S(1)}, f32[4,128,128]{2,1,0:T(8,128)S(1)}, u32[]{:S(2)}, u32[]{:S(2)}) collective-permute-start(f32[4,128,128]{2,1,0:T(8,128)S(1)} %bitcast.11), channel_id=1, source_target_pairs={{4,0},{8,4},{12,8},{16,12},{20,16},{24,20},{28,24},{1,28},{5,1},{9... | collective-permute-start | bytes 786440 | tf_op jit(solution)/shard_map/ppermute | solution.py:68
  29.6 11.9 %collective-permute-start = (f32[3,128,128]{2,1,0:T(8,128)S(1)}, f32[3,128,128]{2,1,0:T(8,128)S(1)}, u32[]{:S(2)}, u32[]{:S(2)}) collective-permute-start(f32[3,128,128]{2,1,0:T(8,128)S(1)} %bitcast.14), channel_id=1, source_target_pairs={{507,0},{511,4},{0,8},{4,12},{8,16},{12,20},{16,24},{20,28},{24,1}... | collective-permute-start | bytes 589832 | tf_op jit(solution)/shard_map/ppermute | solution.py:71
  31.6 12.0 %collective-permute-start.3 = (f32[3,128,128]{2,1,0:T(8,128)S(1)}, f32[3,128,128]{2,1,0:T(8,128)S(1)}, u32[]{:S(2)}, u32[]{:S(2)}) collective-permute-start(f32[3,128,128]{2,1,0:T(8,128)S(1)} %bitcast.13), channel_id=1, source_target_pairs={{8,0},{12,4},{16,8},{20,12},{24,16},{28,20},{1,24},{5,28},{9,1},{1... | collective-permute-start | bytes 589832 | tf_op jit(solution)/shard_map/ppermute | solution.py:70

commit v2 on v1

--- a/solution.py
+++ b/solution.py
@@ -10,16 +10,16 @@
 AXES = ("row", "col", "depth")
 
 
+def place(sizes, i):
+    rows, cols, depths = sizes
+    chunk, col = divmod(i % (rows * cols * depths), cols)
+    row, depth = divmod(chunk, depths)
+    return (row * cols + (cols - 1 - col if chunk % 2 else col)) * depths + depth
+
+
 def ring_pairs(sizes, shift):
-    rows, cols, depths = sizes
-    total = rows * cols * depths
-
-    def place(i):
-        chunk, col = divmod(i % total, cols)
-        row, depth = divmod(chunk, depths)
-        return (row * cols + col) * depths + depth
-
-    return [(place(i + shift), place(i)) for i in range(total)]
+    total = sizes[0] * sizes[1] * sizes[2]
+    return [(place(sizes, i + shift), place(sizes, i)) for i in range(total)]
 
 
 def halves(value):
@@ -31,7 +31,8 @@
     return jnp.dot(left, right, preferred_element_type=jnp.float32)
 
 
-def band_kernel(pattern_ref, own_ref, m2_ref, m1_ref, p1_ref, p2_ref, out_ref):
+def band_kernel(turn_ref, pattern_ref, own_ref, m2_ref, m1_ref, p1_ref, p2_ref, out_ref):
+    parts, _, rows, _ = out_ref.shape
     stored = (m2_ref, m1_ref, own_ref, p1_ref, p2_ref)
     first = (2, 1, 0, 0, 0)
     right = {}
@@ -55,14 +56,20 @@
     square = product([right[HALF, s] for s in range(WIDE)])
     cube = product([halves(block) for block in square])
     for t in range(WIDE):
-        out_ref[:, t] = (3.0 * square[t] - 2.0 * cube[t]).reshape(out_ref.shape[0], -1, out_ref.shape[3])
+        value = 3.0 * square[t] - 2.0 * cube[t]
+        for part in range(parts):
+            out_ref[part ^ turn_ref[0], t] = value[part * rows : (part + 1) * rows]
 
 
 def shards(density, pattern):
     sizes = tuple(lax.axis_size(a) for a in AXES)
     cols, wide, rows, width = density.shape
-    keep = lax.dynamic_index_in_dim(pattern, lax.axis_index("col"), 0, keepdims=False)
-    parts = lax.all_to_all(density, "col", 0, 0, tiled=True)
+    groups = [[place(sizes, i + j) for j in range(cols)] for i in range(0, sizes[0] * sizes[1] * sizes[2], cols)]
+    turned = (lax.axis_index("row") * sizes[2] + lax.axis_index("depth")) % 2
+    turn = turned * (cols - 1)
+    keep = lax.dynamic_index_in_dim(pattern, lax.axis_index("col") ^ turn, 0, keepdims=False)
+    parts = lax.all_to_all(density, AXES, 0, 0, axis_index_groups=groups, tiled=True)
+    parts = jnp.where(turned == 1, jnp.flip(parts, 0), parts)
     own = jnp.swapaxes(parts, 0, 1) * keep.astype(jnp.float32)[:, None, None, None]
     own = own.reshape(wide, cols * rows, width)
     p1 = lax.ppermute(own[:4], AXES, ring_pairs(sizes, 1))
@@ -73,11 +80,11 @@
     result = pl.pallas_call(
         band_kernel,
         out_shape=jax.ShapeDtypeStruct(density.shape, jnp.float32),
-        in_specs=[pl.BlockSpec(memory_space=pltpu.SMEM)] + [vmem] * 5,
+        in_specs=[pl.BlockSpec(memory_space=pltpu.SMEM)] * 2 + [vmem] * 5,
         out_specs=vmem,
         compiler_params=pltpu.CompilerParams(vmem_limit_bytes=32 * 1024 * 1024),
-    )(keep, own, m2, m1, p1, p2)
-    return lax.all_to_all(result, "col", 0, 0, tiled=True)
+    )(turn.reshape(1), keep, own, m2, m1, p1, p2)
+    return lax.all_to_all(result, AXES, 0, 0, axis_index_groups=groups, tiled=True)
 
 
 def solution(mesh):

time: 70.4 us -> 65.3 us (0.928)
  the two profiles are of different devices: /device:TPU:31 before, /device:TPU:38 now
where the time goes in v2:
time: 65.3 us; the launch traced here: 65 us
  starting transfers between devices  25.8 us (40%)
  blocking collectives  18.7 us (29%)
  waiting for transfers between devices  17 us (26%)
  Pallas kernels  1.69 us (3%)
  local copies, waits for them, and re-layouts  0.88 us (1%)
  other arithmetic  0.78 us (1%)
    all_to_all x1, blocking collectives, shards(): lax.all_to_all(result, AXES, 0, 0, axis_index_groups=groups, tiled=True)  18.7 us
    all_to_all x1, starting transfers between devices, shards(): lax.all_to_all(density, AXES, 0, 0, axis_index_groups=groups, tiled=True)  12.4 us
    ppermute x1, waiting for transfers between devices, shards(): m2 = lax.ppermute(own[2:], AXES, ring_pairs(sizes, -2))  9.22 us
    all_to_all x1, waiting for transfers between devices, shards(): lax.all_to_all(density, AXES, 0, 0, axis_index_groups=groups, tiled=True)  7.75 us
    ppermute x1, starting transfers between devices, shards(): p2 = lax.ppermute(own[:3], AXES, ring_pairs(sizes, 2))  4.84 us
    ppermute x1, starting transfers between devices, shards(): p1 = lax.ppermute(own[:4], AXES, ring_pairs(sizes, 1))  3.71 us
    ppermute x1, starting transfers between devices, shards(): m1 = lax.ppermute(own[1:], AXES, ring_pairs(sizes, -1))  2.92 us
    ppermute x1, starting transfers between devices, shards(): m2 = lax.ppermute(own[2:], AXES, ring_pairs(sizes, -2))  1.92 us
  transfers between devices with their start and end apart: 5, of which 2 were waited for; matrix products, arithmetic and copies ran while one was open for 1% of the time, Pallas kernels for 0%

profile of v2, /device:TPU:38, one launch (start us, length us, event | category | flops | bytes accessed | tf_op | source)
XLA Modules:
  0.0 65.0 jit_solution(4272853839377158964)
XLA Ops:
  0.0 12.4 %all-to-all-start = ((f32[8,5,16,128]{3,2,1,0:T(8,128)}), f32[8,5,16,128]{3,2,1,0:T(8,128)S(1)}, u32[]{:S(2)}, u32[]{:S(2)}) async-start(f32[8,5,16,128]{3,2,1,0:T(8,128)} %param.2), calls=%async_computation | async-start | bytes 655360 | tf_op jit(solution)/shard_map/all_to_all | solution.py:71
  12.4 0.7 %fusion.2 = (f32[5]{0:T(128)S(1)}, s32[5]{0:T(128)S(1)}) fusion(s32[8,5]{1,0:T(8,128)} %param.3, s32[]{:T(128)S(6)} %select_n.20), kind=kLoop, calls=%fused_computation.4 | loop fusion | flops 5 | bytes 64 | tf_op jit(solution)/shard_map/convert_element_type | solution.py:73
  13.1 7.8 %all-to-all-done = f32[8,5,16,128]{3,2,1,0:T(8,128)S(1)} async-done(((f32[8,5,16,128]{3,2,1,0:T(8,128)}), f32[8,5,16,128]{3,2,1,0:T(8,128)S(1)}, u32[]{:S(2)}, u32[]{:S(2)}) %all-to-all-start) | async-done | bytes 327712 | tf_op jit(solution)/shard_map/all_to_all | solution.py:71
  20.9 0.1 fusion.1
  21.1 2.9 %collective-permute-start.1 = (f32[4,128,128]{2,1,0:T(8,128)S(1)}, f32[4,128,128]{2,1,0:T(8,128)S(1)}, u32[]{:S(2)}, u32[]{:S(2)}) collective-permute-start(f32[4,128,128]{2,1,0:T(8,128)S(1)} %bitcast.13), channel_id=1, source_target_pairs={{483,0},{0,4},{4,8},{8,12},{12,16},{16,20},{20,24},{24,28},{28,29}... | collective-permute-start | bytes 786440 | tf_op jit(solution)/shard_map/ppermute | solution.py:76
  24.0 3.7 %collective-permute-start.2 = (f32[4,128,128]{2,1,0:T(8,128)S(1)}, f32[4,128,128]{2,1,0:T(8,128)S(1)}, u32[]{:S(2)}, u32[]{:S(2)}) collective-permute-start(f32[4,128,128]{2,1,0:T(8,128)S(1)} %bitcast.12), channel_id=1, source_target_pairs={{4,0},{8,4},{12,8},{16,12},{20,16},{24,20},{28,24},{29,28},{25,29}... | collective-permute-start | bytes 786440 | tf_op jit(solution)/shard_map/ppermute | solution.py:75
  27.8 1.9 %collective-permute-start = (f32[3,128,128]{2,1,0:T(8,128)S(1)}, f32[3,128,128]{2,1,0:T(8,128)S(1)}, u32[]{:S(2)}, u32[]{:S(2)}) collective-permute-start(f32[3,128,128]{2,1,0:T(8,128)S(1)} %bitcast.15), channel_id=1, source_target_pairs={{487,0},{483,4},{0,8},{4,12},{8,16},{12,20},{16,24},{20,28},{24,29... | collective-permute-start | bytes 589832 | tf_op jit(solution)/shard_map/ppermute | solution.py:78
  29.7 4.8 %collective-permute-start.3 = (f32[3,128,128]{2,1,0:T(8,128)S(1)}, f32[3,128,128]{2,1,0:T(8,128)S(1)}, u32[]{:S(2)}, u32[]{:S(2)}) collective-permute-start(f32[3,128,128]{2,1,0:T(8,128)S(1)} %bitcast.14), channel_id=1, source_target_pairs={{8,0},{12,4},{16,8},{20,12},{24,16},{28,20},{29,24},{25,28},{21,29... | collective-permute-start | bytes 589832 | tf_op jit(solution)/shard_map/ppermute | solution.py:77
  34.6 9.2 %collective-permute-done.m2_ref = f32[3,128,128]{2,1,0:T(8,128)S(1)} collective-permute-done((f32[3,128,128]{2,1,0:T(8,128)S(1)}, f32[3,128,128]{2,1,0:T(8,128)S(1)}, u32[]{:S(2)}, u32[]{:S(2)}) %collective-permute-start) | collective-permute-done | bytes 196640 | tf_op jit(solution)/shard_map/ppermute | solution.py:78
  43.8 0.0 collective-permute-done.3.p2_ref
  43.8 0.0 collective-permute-done.1.m1_ref
  43.8 0.0 collective-permute-done.2.p1_ref
  43.8 1.7 %shard_map.28 = f32[8,5,16,128]{3,2,1,0:T(8,128)S(1)} custom-call(s32[1]{0:T(128)} %bitcast.turn_ref, s32[5]{0:T(128)S(1)} %get-tuple-element.6.pattern_ref, f32[5,128,128]{2,1,0:T(8,128)S(1)} %bitcast.11, f32[3,128,128]{2,1,0:T(8,128)S(1)} %collective-permute-done.m2_ref, f32[4,128,128]{2,1,0:T(8,128)S(1)} %collective-permute-done.1.m1_ref, ...), custom_call_target="tpu_custom_call" | custom-call | tf_op jit(solution)/shard_map/pallas_call | solution.py:80
  45.5 18.7 %all_to_all.10 = f32[8,5,16,128]{3,2,1,0:T(8,128)S(1)} all-to-all(f32[8,5,16,128]{3,2,1,0:T(8,128)S(1)} %shard_map.28), channel_id=1, replica_groups={{0,4,8,12,16,20,24,28},{29,25,21,17,13,9,5,1},{2,6,10,14,18,22,26,30},{..., dimensions={0} | all-to-all | bytes 655360 | tf_op jit(solution)/shard_map/all_to_all | solution.py:87
  64.2 0.7 %copy.9 = f32[8,5,16,128]{3,2,1,0:T(8,128)} copy(f32[8,5,16,128]{3,2,1,0:T(8,128)S(1)} %all_to_all.10) | data formatting | bytes 655360
  (7 shorter events, 0.2 us)
Async XLA Ops:
  0.0 20.9 %all-to-all-start = ((f32[8,5,16,128]{3,2,1,0:T(8,128)}), f32[8,5,16,128]{3,2,1,0:T(8,128)S(1)}, u32[]{:S(2)}, u32[]{:S(2)}) async-start(f32[8,5,16,128]{3,2,1,0:T(8,128)} %param.2), calls=%async_computation | async-start | bytes 655360 | tf_op jit(solution)/shard_map/all_to_all | solution.py:71
  21.1 22.8 %collective-permute-start.1 = (f32[4,128,128]{2,1,0:T(8,128)S(1)}, f32[4,128,128]{2,1,0:T(8,128)S(1)}, u32[]{:S(2)}, u32[]{:S(2)}) collective-permute-start(f32[4,128,128]{2,1,0:T(8,128)S(1)} %bitcast.13), channel_id=1, source_target_pairs={{483,0},{0,4},{4,8},{8,12},{12,16},{16,20},{20,24},{24,28},{28,29}... | collective-permute-start | bytes 786440 | tf_op jit(solution)/shard_map/ppermute | solution.py:76
  24.0 19.8 %collective-permute-start.2 = (f32[4,128,128]{2,1,0:T(8,128)S(1)}, f32[4,128,128]{2,1,0:T(8,128)S(1)}, u32[]{:S(2)}, u32[]{:S(2)}) collective-permute-start(f32[4,128,128]{2,1,0:T(8,128)S(1)} %bitcast.12), channel_id=1, source_target_pairs={{4,0},{8,4},{12,8},{16,12},{20,16},{24,20},{28,24},{29,28},{25,29}... | collective-permute-start | bytes 786440 | tf_op jit(solution)/shard_map/ppermute | solution.py:75
  27.8 16.0 %collective-permute-start = (f32[3,128,128]{2,1,0:T(8,128)S(1)}, f32[3,128,128]{2,1,0:T(8,128)S(1)}, u32[]{:S(2)}, u32[]{:S(2)}) collective-permute-start(f32[3,128,128]{2,1,0:T(8,128)S(1)} %bitcast.15), channel_id=1, source_target_pairs={{487,0},{483,4},{0,8},{4,12},{8,16},{12,20},{16,24},{20,28},{24,29... | collective-permute-start | bytes 589832 | tf_op jit(solution)/shard_map/ppermute | solution.py:78
  29.7 14.1 %collective-permute-start.3 = (f32[3,128,128]{2,1,0:T(8,128)S(1)}, f32[3,128,128]{2,1,0:T(8,128)S(1)}, u32[]{:S(2)}, u32[]{:S(2)}) collective-permute-start(f32[3,128,128]{2,1,0:T(8,128)S(1)} %bitcast.14), channel_id=1, source_target_pairs={{8,0},{12,4},{16,8},{20,12},{24,16},{28,20},{29,24},{25,28},{21,29... | collective-permute-start | bytes 589832 | tf_op jit(solution)/shard_map/ppermute | solution.py:77

commit v3 on v2

v3 whole, which is shorter than its diff:
```python
import jax
import jax.numpy as jnp
from jax import lax
from jax.experimental import pallas as pl
from jax.experimental.pallas import tpu as pltpu
from jax.sharding import PartitionSpec as P

HALF = 2
WIDE = 5
AXES = ("row", "col", "depth")
VMEM = pl.BlockSpec(memory_space=pltpu.VMEM)
PARAMS = pltpu.CompilerParams(vmem_limit_bytes=32 * 1024 * 1024)


def owner(sizes, i):
    rows, cols, depths = sizes
    chunk, col = divmod(i % (rows * cols * depths), cols)
    row, depth = divmod(chunk, depths)
    return (row * cols + (cols - 1 - col if chunk % 2 else col)) * depths + depth


def exchange(sizes, first):
    result = []
    for i in range(first, sizes[0] * sizes[1] * sizes[2], 2):
        a, b = owner(sizes, i), owner(sizes, i + 1)
        result += [(a, b), (b, a)]
    return result


def place():
    chunk = lax.axis_index("row") * lax.axis_size("depth") + lax.axis_index("depth")
    flip = (chunk & 1) * (lax.axis_size("col") - 1)
    return flip, lax.axis_index("col") ^ flip


def halves(value):
    high = value.astype(jnp.bfloat16)
    return high, (value - high.astype(jnp.float32)).astype(jnp.bfloat16)


def dot(left, right):
    return jnp.dot(left, right, preferred_element_type=jnp.float32)


def arrange_kernel(marks_ref, parts_ref, own_ref, near_ref, far_ref):
    parts, _, rows, _ = parts_ref.shape
    flip, row = place()
    odd = row & 1
    for slot in range(WIDE):
        keep = marks_ref[pl.ds(row, 1), slot : slot + 1]
        for part in range(parts):
            own_ref[slot, part * rows : (part + 1) * rows] = parts_ref[part ^ flip, slot] * keep
    for slot in range(WIDE - 1):
        near_ref[slot] = own_ref[slot + 1 - odd]
        far_ref[slot] = own_ref[slot + odd]


def band_kernel(marks_ref, own_ref, near_ref, far_ref, relayed_ref, handed_ref, out_ref):
    parts, _, rows, _ = out_ref.shape
    flip, row = place()
    even = row & 1 == 0
    right = {(HALF, s): halves(own_ref[s]) for s in range(WIDE)}
    for s in range(WIDE - 1):
        near, far = near_ref[s], far_ref[s]
        right[HALF + 1, s] = halves(jnp.where(even, near, far))
        right[HALF - 1, s + 1] = halves(jnp.where(even, far, near))
    for s in range(WIDE - 2):
        relayed, handed = relayed_ref[s], handed_ref[s]
        right[HALF + 2, s] = halves(jnp.where(even, handed, relayed))
        right[HALF - 2, s + 2] = halves(jnp.where(even, relayed, handed))
    keep = [marks_ref[pl.ds(row, 1), t : t + 1] for t in range(WIDE)]

    def product(left):
        result = []
        for t in range(WIDE):
            summed = None
            for u in range(max(0, t - HALF), min(WIDE, t + HALF + 1)):
                high, low = left[u]
                other_high, other_low = right[u, t - u + HALF]
                term = dot(high, other_high) + dot(high, other_low) + dot(low, other_high)
                summed = term if summed is None else summed + term
            result.append(summed * keep[t])
        return result

    square = product([right[HALF, s] for s in range(WIDE)])
    cube = product([halves(block) for block in square])
    for t in range(WIDE):
        value = 3.0 * square[t] - 2.0 * cube[t]
        for part in range(parts):
            out_ref[part ^ flip, t] = value[part * rows : (part + 1) * rows]


def shards(density, pattern):
    sizes = tuple(lax.axis_size(a) for a in AXES)
    cols, wide, rows, width = density.shape
    groups = [[owner(sizes, i + j) for j in range(cols)] for i in range(0, sizes[0] * sizes[1] * sizes[2], cols)]
    inside, outside = exchange(sizes, 0), exchange(sizes, 1)
    odd = place()[1] & 1

    def blocks(n):
        return jax.ShapeDtypeStruct((n, cols * rows, width), jnp.float32)

    parts = lax.all_to_all(density, AXES, 0, 0, axis_index_groups=groups, tiled=True)
    marks = jnp.pad(pattern.astype(jnp.float32), ((0, 0), (0, width - wide)))
    own, near, far = pl.pallas_call(
        arrange_kernel,
        out_shape=(blocks(wide), blocks(wide - 1), blocks(wide - 1)),
        in_specs=[VMEM] * 2,
        out_specs=(VMEM,) * 3,
        compiler_params=PARAMS,
    )(marks, parts)
    far = lax.ppermute(far, AXES, outside)
    near = lax.ppermute(near, AXES, inside)
    relayed = lax.ppermute(lax.dynamic_slice_in_dim(near, odd, wide - 2, 0), AXES, outside)
    handed = lax.ppermute(lax.dynamic_slice_in_dim(far, 1 - odd, wide - 2, 0), AXES, inside)
    result = pl.pallas_call(
        band_kernel,
        out_shape=jax.ShapeDtypeStruct(density.shape, jnp.float32),
        in_specs=[VMEM] * 6,
        out_specs=VMEM,
        compiler_params=PARAMS,
    )(marks, own, near, far, relayed, handed)
    return lax.all_to_all(result, AXES, 0, 0, axis_index_groups=groups, tiled=True)


def solution(mesh):
    in_specs = (P(("row", "depth"), None, "col", None), P(("row", "depth"), None))
    out_specs = P(("row", "depth"), None, "col", None)
    return jax.shard_map(shards, mesh=mesh, in_specs=in_specs, out_specs=out_specs, check_vma=False)
```

time: 65.3 us -> 64.2 us (0.983)
  the two profiles are of different devices: /device:TPU:38 before, /device:TPU:56 now
where the time goes in v3:
time: 64.2 us; the launch traced here: 63.9 us
  starting transfers between devices  23.6 us (37%)
  waiting for transfers between devices  21.9 us (34%)
  blocking collectives  16.2 us (25%)
  Pallas kernels  1.36 us (2%)
  local copies, waits for them, and re-layouts  0.76 us (1%)
    all_to_all x1, blocking collectives, shards(): lax.all_to_all(result, AXES, 0, 0, axis_index_groups=groups, tiled=True)  16.2 us
    all_to_all x1, waiting for transfers between devices, shards(): lax.all_to_all(density, AXES, 0, 0, axis_index_groups=groups, tiled=True)  13.3 us
    all_to_all x1, starting transfers between devices, shards(): lax.all_to_all(density, AXES, 0, 0, axis_index_groups=groups, tiled=True)  10.4 us
    ppermute x1, waiting for transfers between devices, shards(): lax.ppermute(lax.dynamic_slice_in_dim(far, 1 - odd, wide - 2, 0), AXES, i...  4.3 us
    ppermute x1, starting transfers between devices, shards(): lax.ppermute(lax.dynamic_slice_in_dim(far, 1 - odd, wide - 2, 0), AXES, i...  3.83 us
    ppermute x1, starting transfers between devices, shards(): far = lax.ppermute(far, AXES, outside)  3.59 us
    ppermute x1, starting transfers between devices, shards(): lax.ppermute(lax.dynamic_slice_in_dim(near, odd, wide - 2, 0), AXES, outs...  3.21 us
    ppermute x1, starting transfers between devices, shards(): near = lax.ppermute(near, AXES, inside)  2.47 us
  transfers between devices with their start and end apart: 5, of which 5 were waited for; matrix products, arithmetic and copies ran while one was open for 0% of the time, Pallas kernels for 0%

profile of v3, /device:TPU:56, one launch (start us, length us, event | category | flops | bytes accessed | tf_op | source)
XLA Modules:
  0.0 63.9 jit_solution(4412460165839464466)
XLA Ops:
  0.0 0.0 copy-start
  0.0 10.4 %all-to-all-start = ((f32[8,5,16,128]{3,2,1,0:T(8,128)}), f32[8,5,16,128]{3,2,1,0:T(8,128)S(1)}, u32[]{:S(2)}, u32[]{:S(2)}) async-start(f32[8,5,16,128]{3,2,1,0:T(8,128)} %param.2), calls=%async_computation | async-start | bytes 655360 | tf_op jit(solution)/shard_map/all_to_all | solution.py:103
  10.5 0.0 copy-done
  10.5 13.3 %all-to-all-done.parts_ref = f32[8,5,16,128]{3,2,1,0:T(8,128)S(1)} async-done(((f32[8,5,16,128]{3,2,1,0:T(8,128)}), f32[8,5,16,128]{3,2,1,0:T(8,128)S(1)}, u32[]{:S(2)}, u32[]{:S(2)}) %all-to-all-start) | async-done | bytes 327712 | tf_op jit(solution)/shard_map/all_to_all | solution.py:103
  23.7 0.2 shard_map.28
  23.9 2.5 %collective-permute-start = (f32[4,128,128]{2,1,0:T(8,128)S(1)}, f32[4,128,128]{2,1,0:T(8,128)S(1)}, u32[]{:S(2)}, u32[]{:S(2)}) collective-permute-start(f32[4,128,128]{2,1,0:T(8,128)S(1)} %get-tuple-element.9), channel_id=1, source_target_pairs={{0,4},{4,0},{8,12},{12,8},{16,20},{20,16},{24,28},{28,24},{29,25},... | collective-permute-start | bytes 786440 | tf_op jit(solution)/shard_map/ppermute | solution.py:113
  26.4 3.6 %collective-permute-start.1 = (f32[4,128,128]{2,1,0:T(8,128)S(1)}, f32[4,128,128]{2,1,0:T(8,128)S(1)}, u32[]{:S(2)}, u32[]{:S(2)}) collective-permute-start(f32[4,128,128]{2,1,0:T(8,128)S(1)} %get-tuple-element.10), channel_id=1, source_target_pairs={{4,8},{8,4},{12,16},{16,12},{20,24},{24,20},{28,29},{29,28},{25,21... | collective-permute-start | bytes 786440 | tf_op jit(solution)/shard_map/ppermute | solution.py:112
  30.0 2.2 %collective-permute-done.near_ref = f32[4,128,128]{2,1,0:T(8,128)S(1)} collective-permute-done((f32[4,128,128]{2,1,0:T(8,128)S(1)}, f32[4,128,128]{2,1,0:T(8,128)S(1)}, u32[]{:S(2)}, u32[]{:S(2)}) %collective-permute-start) | collective-permute-done | bytes 262176 | tf_op jit(solution)/shard_map/ppermute | solution.py:113
  32.2 3.2 %collective-permute-start.2 = (f32[3,128,128]{2,1,0:T(8,128)S(1)}, f32[3,128,128]{2,1,0:T(8,128)S(1)}, u32[]{:S(2)}, u32[]{:S(2)}) collective-permute-start(f32[3,128,128]{2,1,0:T(8,128)S(1)} %constant_dynamic-slice_fusion.1), channel_id=1, source_target_pairs={{4,8},{8,4},{12,16},{16,12},{20,24},{24,20},{28,29},{29,28},{25,21... | collective-permute-start | bytes 589832 | tf_op jit(solution)/shard_map/ppermute | solution.py:114
  35.4 0.9 %collective-permute-done.1.far_ref = f32[4,128,128]{2,1,0:T(8,128)S(1)} collective-permute-done((f32[4,128,128]{2,1,0:T(8,128)S(1)}, f32[4,128,128]{2,1,0:T(8,128)S(1)}, u32[]{:S(2)}, u32[]{:S(2)}) %collective-permute-start.1) | collective-permute-done | bytes 262176 | tf_op jit(solution)/shard_map/ppermute | solution.py:112
  36.3 3.8 %collective-permute-start.3 = (f32[3,128,128]{2,1,0:T(8,128)S(1)}, f32[3,128,128]{2,1,0:T(8,128)S(1)}, u32[]{:S(2)}, u32[]{:S(2)}) collective-permute-start(f32[3,128,128]{2,1,0:T(8,128)S(1)} %constant_dynamic-slice_fusion), channel_id=1, source_target_pairs={{0,4},{4,0},{8,12},{12,8},{16,20},{20,16},{24,28},{28,24},{29,25},... | collective-permute-start | bytes 589832 | tf_op jit(solution)/shard_map/ppermute | solution.py:115
  40.2 1.3 %collective-permute-done.2.relayed_ref = f32[3,128,128]{2,1,0:T(8,128)S(1)} collective-permute-done((f32[3,128,128]{2,1,0:T(8,128)S(1)}, f32[3,128,128]{2,1,0:T(8,128)S(1)}, u32[]{:S(2)}, u32[]{:S(2)}) %collective-permute-start.2) | collective-permute-done | bytes 196640 | tf_op jit(solution)/shard_map/ppermute | solution.py:114
  41.4 4.3 %collective-permute-done.3.handed_ref = f32[3,128,128]{2,1,0:T(8,128)S(1)} collective-permute-done((f32[3,128,128]{2,1,0:T(8,128)S(1)}, f32[3,128,128]{2,1,0:T(8,128)S(1)}, u32[]{:S(2)}, u32[]{:S(2)}) %collective-permute-start.3) | collective-permute-done | bytes 196640 | tf_op jit(solution)/shard_map/ppermute | solution.py:115
  45.7 1.2 %shard_map.29 = f32[8,5,16,128]{3,2,1,0:T(8,128)S(1)} custom-call(f32[8,128]{1,0:T(8,128)S(1)} %pad.4.marks_ref, f32[5,128,128]{2,1,0:T(8,128)S(1)} %get-tuple-element.8.own_ref, f32[4,128,128]{2,1,0:T(8,128)S(1)} %collective-permute-done.near_ref, f32[4,128,128]{2,1,0:T(8,128)S(1)} %collective-permute-done.1.far_ref, ...), custom_call_target="tpu_custom_call" | custom-call | tf_op jit(solution)/shard_map/pallas_call | solution.py:116
  46.9 16.2 %all_to_all.10 = f32[8,5,16,128]{3,2,1,0:T(8,128)S(1)} all-to-all(f32[8,5,16,128]{3,2,1,0:T(8,128)S(1)} %shard_map.29), channel_id=1, replica_groups={{0,4,8,12,16,20,24,28},{29,25,21,17,13,9,5,1},{2,6,10,14,18,22,26,30},{..., dimensions={0} | all-to-all | bytes 655360 | tf_op jit(solution)/shard_map/all_to_all | solution.py:123
  63.1 0.7 %copy.4 = f32[8,5,16,128]{3,2,1,0:T(8,128)} copy(f32[8,5,16,128]{3,2,1,0:T(8,128)S(1)} %all_to_all.10) | data formatting | bytes 655360
  (4 shorter events, 0.0 us)
Async XLA Ops:
  0.0 10.5 %copy-start = (s32[8,5]{1,0:T(8,128)S(1)}, s32[8,5]{1,0:T(8,128)}, u32[]{:S(2)}) copy-start(s32[8,5]{1,0:T(8,128)} %param.3) | copy-start | bytes 484
  0.0 23.7 %all-to-all-start = ((f32[8,5,16,128]{3,2,1,0:T(8,128)}), f32[8,5,16,128]{3,2,1,0:T(8,128)S(1)}, u32[]{:S(2)}, u32[]{:S(2)}) async-start(f32[8,5,16,128]{3,2,1,0:T(8,128)} %param.2), calls=%async_computation | async-start | bytes 655360 | tf_op jit(solution)/shard_map/all_to_all | solution.py:103
  23.9 8.3 %collective-permute-start = (f32[4,128,128]{2,1,0:T(8,128)S(1)}, f32[4,128,128]{2,1,0:T(8,128)S(1)}, u32[]{:S(2)}, u32[]{:S(2)}) collective-permute-start(f32[4,128,128]{2,1,0:T(8,128)S(1)} %get-tuple-element.9), channel_id=1, source_target_pairs={{0,4},{4,0},{8,12},{12,8},{16,20},{20,16},{24,28},{28,24},{29,25},... | collective-permute-start | bytes 786440 | tf_op jit(solution)/shard_map/ppermute | solution.py:113
  26.4 9.9 %collective-permute-start.1 = (f32[4,128,128]{2,1,0:T(8,128)S(1)}, f32[4,128,128]{2,1,0:T(8,128)S(1)}, u32[]{:S(2)}, u32[]{:S(2)}) collective-permute-start(f32[4,128,128]{2,1,0:T(8,128)S(1)} %get-tuple-element.10), channel_id=1, source_target_pairs={{4,8},{8,4},{12,16},{16,12},{20,24},{24,20},{28,29},{29,28},{25,21... | collective-permute-start | bytes 786440 | tf_op jit(solution)/shard_map/ppermute | solution.py:112
  32.2 9.2 %collective-permute-start.2 = (f32[3,128,128]{2,1,0:T(8,128)S(1)}, f32[3,128,128]{2,1,0:T(8,128)S(1)}, u32[]{:S(2)}, u32[]{:S(2)}) collective-permute-start(f32[3,128,128]{2,1,0:T(8,128)S(1)} %constant_dynamic-slice_fusion.1), channel_id=1, source_target_pairs={{4,8},{8,4},{12,16},{16,12},{20,24},{24,20},{28,29},{29,28},{25,21... | collective-permute-start | bytes 589832 | tf_op jit(solution)/shard_map/ppermute | solution.py:114
  36.3 9.4 %collective-permute-start.3 = (f32[3,128,128]{2,1,0:T(8,128)S(1)}, f32[3,128,128]{2,1,0:T(8,128)S(1)}, u32[]{:S(2)}, u32[]{:S(2)}) collective-permute-start(f32[3,128,128]{2,1,0:T(8,128)S(1)} %constant_dynamic-slice_fusion), channel_id=1, source_target_pairs={{0,4},{4,0},{8,12},{12,8},{16,20},{20,16},{24,28},{28,24},{29,25},... | collective-permute-start | bytes 589832 | tf_op jit(solution)/shard_map/ppermute | solution.py:115

commit v4 on v3

--- a/solution.py
+++ b/solution.py
@@ -8,15 +8,18 @@
 HALF = 2
 WIDE = 5
 AXES = ("row", "col", "depth")
+START = 4
+TURNED = 1
 VMEM = pl.BlockSpec(memory_space=pltpu.VMEM)
 PARAMS = pltpu.CompilerParams(vmem_limit_bytes=32 * 1024 * 1024)
 
 
 def owner(sizes, i):
     rows, cols, depths = sizes
-    chunk, col = divmod(i % (rows * cols * depths), cols)
+    chunk, at = divmod(i % (rows * cols * depths), cols)
     row, depth = divmod(chunk, depths)
-    return (row * cols + (cols - 1 - col if chunk % 2 else col)) * depths + depth
+    col = (START + (cols - 1 - at if chunk % 2 == TURNED else at)) % cols
+    return (row * cols + col) * depths + depth
 
 
 def exchange(sizes, first):
@@ -28,9 +31,10 @@
 
 
 def place():
+    cols = lax.axis_size("col")
     chunk = lax.axis_index("row") * lax.axis_size("depth") + lax.axis_index("depth")
-    flip = (chunk & 1) * (lax.axis_size("col") - 1)
-    return flip, lax.axis_index("col") ^ flip
+    flip = jnp.where((chunk & 1) == TURNED, cols - 1, 0)
+    return flip, ((lax.axis_index("col") + cols - START) % cols) ^ flip
 
 
 def halves(value):
@@ -49,7 +53,7 @@
     for slot in range(WIDE):
         keep = marks_ref[pl.ds(row, 1), slot : slot + 1]
         for part in range(parts):
-            own_ref[slot, part * rows : (part + 1) * rows] = parts_ref[part ^ flip, slot] * keep
+            own_ref[slot, part * rows : (part + 1) * rows] = parts_ref[(part - START) % parts ^ flip, slot] * keep
     for slot in range(WIDE - 1):
         near_ref[slot] = own_ref[slot + 1 - odd]
         far_ref[slot] = own_ref[slot + odd]
@@ -87,7 +91,7 @@
     for t in range(WIDE):
         value = 3.0 * square[t] - 2.0 * cube[t]
         for part in range(parts):
-            out_ref[part ^ flip, t] = value[part * rows : (part + 1) * rows]
+            out_ref[(part - START) % parts ^ flip, t] = value[part * rows : (part + 1) * rows]
 
 
 def shards(density, pattern):

time: 64.2 us -> 62.6 us (0.975)
  the two profiles are of different devices: /device:TPU:56 before, /device:TPU:1 now
where the time goes in v4:
time: 62.6 us; the launch traced here: 61.4 us
  starting transfers between devices  27.1 us (43%)
  blocking collectives  19.1 us (31%)
  waiting for transfers between devices  13 us (21%)
  Pallas kernels  1.36 us (2%)
  local copies, waits for them, and re-layouts  0.77 us (1%)
    all_to_all x1, blocking collectives, shards(): lax.all_to_all(result, AXES, 0, 0, axis_index_groups=groups, tiled=True)  19.1 us
    all_to_all x1, starting transfers between devices, shards(): lax.all_to_all(density, AXES, 0, 0, axis_index_groups=groups, tiled=True)  14 us
    all_to_all x1, waiting for transfers between devices, shards(): lax.all_to_all(density, AXES, 0, 0, axis_index_groups=groups, tiled=True)  7.49 us
    ppermute x1, starting transfers between devices, shards(): far = lax.ppermute(far, AXES, outside)  4.47 us
    ppermute x1, starting transfers between devices, shards(): lax.ppermute(lax.dynamic_slice_in_dim(near, odd, wide - 2, 0), AXES, outs...  3.97 us
    ppermute x1, waiting for transfers between devices, shards(): lax.ppermute(lax.dynamic_slice_in_dim(far, 1 - odd, wide - 2, 0), AXES, i...  2.87 us
    ppermute x1, starting transfers between devices, shards(): lax.ppermute(lax.dynamic_slice_in_dim(far, 1 - odd, wide - 2, 0), AXES, i...  2.82 us
    ppermute x1, starting transfers between devices, shards(): near = lax.ppermute(near, AXES, inside)  1.92 us
  transfers between devices with their start and end apart: 5, of which 4 were waited for; matrix products, arithmetic and copies ran while one was open for 0% of the time, Pallas kernels for 0%

profile of v4, /device:TPU:1, one launch (start us, length us, event | category | flops | bytes accessed | tf_op | source)
XLA Modules:
  0.0 61.4 jit_solution(7673228895496345522)
XLA Ops:
  0.0 0.0 copy-start
  0.0 14.0 %all-to-all-start = ((f32[8,5,16,128]{3,2,1,0:T(8,128)}), f32[8,5,16,128]{3,2,1,0:T(8,128)S(1)}, u32[]{:S(2)}, u32[]{:S(2)}) async-start(f32[8,5,16,128]{3,2,1,0:T(8,128)} %param.2), calls=%async_computation | async-start | bytes 655360 | tf_op jit(solution)/shard_map/all_to_all | solution.py:107
  14.0 0.0 copy-done
  14.0 7.5 %all-to-all-done.parts_ref = f32[8,5,16,128]{3,2,1,0:T(8,128)S(1)} async-done(((f32[8,5,16,128]{3,2,1,0:T(8,128)}), f32[8,5,16,128]{3,2,1,0:T(8,128)S(1)}, u32[]{:S(2)}, u32[]{:S(2)}) %all-to-all-start) | async-done | bytes 327712 | tf_op jit(solution)/shard_map/all_to_all | solution.py:107
  21.5 0.2 shard_map.28
  21.7 1.9 %collective-permute-start = (f32[4,128,128]{2,1,0:T(8,128)S(1)}, f32[4,128,128]{2,1,0:T(8,128)S(1)}, u32[]{:S(2)}, u32[]{:S(2)}) collective-permute-start(f32[4,128,128]{2,1,0:T(8,128)S(1)} %get-tuple-element.9), channel_id=1, source_target_pairs={{16,20},{20,16},{24,28},{28,24},{0,4},{4,0},{8,12},{12,8},{13,9},{... | collective-permute-start | bytes 786440 | tf_op jit(solution)/shard_map/ppermute | solution.py:117
  23.6 4.5 %collective-permute-start.1 = (f32[4,128,128]{2,1,0:T(8,128)S(1)}, f32[4,128,128]{2,1,0:T(8,128)S(1)}, u32[]{:S(2)}, u32[]{:S(2)}) collective-permute-start(f32[4,128,128]{2,1,0:T(8,128)S(1)} %get-tuple-element.10), channel_id=1, source_target_pairs={{20,24},{24,20},{28,0},{0,28},{4,8},{8,4},{12,13},{13,12},{9,5},{5... | collective-permute-start | bytes 786440 | tf_op jit(solution)/shard_map/ppermute | solution.py:116
  28.1 1.6 %collective-permute-done.near_ref = f32[4,128,128]{2,1,0:T(8,128)S(1)} collective-permute-done((f32[4,128,128]{2,1,0:T(8,128)S(1)}, f32[4,128,128]{2,1,0:T(8,128)S(1)}, u32[]{:S(2)}, u32[]{:S(2)}) %collective-permute-start) | collective-permute-done | bytes 262176 | tf_op jit(solution)/shard_map/ppermute | solution.py:117
  29.7 4.0 %collective-permute-start.2 = (f32[3,128,128]{2,1,0:T(8,128)S(1)}, f32[3,128,128]{2,1,0:T(8,128)S(1)}, u32[]{:S(2)}, u32[]{:S(2)}) collective-permute-start(f32[3,128,128]{2,1,0:T(8,128)S(1)} %constant_dynamic-slice_fusion.1), channel_id=1, source_target_pairs={{20,24},{24,20},{28,0},{0,28},{4,8},{8,4},{12,13},{13,12},{9,5},{5... | collective-permute-start | bytes 589832 | tf_op jit(solution)/shard_map/ppermute | solution.py:118
  33.7 0.0 collective-permute-done.1.far_ref
  33.7 2.8 %collective-permute-start.3 = (f32[3,128,128]{2,1,0:T(8,128)S(1)}, f32[3,128,128]{2,1,0:T(8,128)S(1)}, u32[]{:S(2)}, u32[]{:S(2)}) collective-permute-start(f32[3,128,128]{2,1,0:T(8,128)S(1)} %constant_dynamic-slice_fusion), channel_id=1, source_target_pairs={{16,20},{20,16},{24,28},{28,24},{0,4},{4,0},{8,12},{12,8},{13,9},{... | collective-permute-start | bytes 589832 | tf_op jit(solution)/shard_map/ppermute | solution.py:119
  36.6 1.0 %collective-permute-done.2.relayed_ref = f32[3,128,128]{2,1,0:T(8,128)S(1)} collective-permute-done((f32[3,128,128]{2,1,0:T(8,128)S(1)}, f32[3,128,128]{2,1,0:T(8,128)S(1)}, u32[]{:S(2)}, u32[]{:S(2)}) %collective-permute-start.2) | collective-permute-done | bytes 196640 | tf_op jit(solution)/shard_map/ppermute | solution.py:118
  37.6 2.9 %collective-permute-done.3.handed_ref = f32[3,128,128]{2,1,0:T(8,128)S(1)} collective-permute-done((f32[3,128,128]{2,1,0:T(8,128)S(1)}, f32[3,128,128]{2,1,0:T(8,128)S(1)}, u32[]{:S(2)}, u32[]{:S(2)}) %collective-permute-start.3) | collective-permute-done | bytes 196640 | tf_op jit(solution)/shard_map/ppermute | solution.py:119
  40.4 1.2 %shard_map.29 = f32[8,5,16,128]{3,2,1,0:T(8,128)S(1)} custom-call(f32[8,128]{1,0:T(8,128)S(1)} %pad.4.marks_ref, f32[5,128,128]{2,1,0:T(8,128)S(1)} %get-tuple-element.8.own_ref, f32[4,128,128]{2,1,0:T(8,128)S(1)} %collective-permute-done.near_ref, f32[4,128,128]{2,1,0:T(8,128)S(1)} %collective-permute-done.1.far_ref, ...), custom_call_target="tpu_custom_call" | custom-call | tf_op jit(solution)/shard_map/pallas_call | solution.py:120
  41.7 19.1 %all_to_all.10 = f32[8,5,16,128]{3,2,1,0:T(8,128)S(1)} all-to-all(f32[8,5,16,128]{3,2,1,0:T(8,128)S(1)} %shard_map.29), channel_id=1, replica_groups={{16,20,24,28,0,4,8,12},{13,9,5,1,29,25,21,17},{18,22,26,30,2,6,10,14},{..., dimensions={0} | all-to-all | bytes 655360 | tf_op jit(solution)/shard_map/all_to_all | solution.py:127
  60.7 0.7 %copy.4 = f32[8,5,16,128]{3,2,1,0:T(8,128)} copy(f32[8,5,16,128]{3,2,1,0:T(8,128)S(1)} %all_to_all.10) | data formatting | bytes 655360
  (4 shorter events, 0.0 us)
Async XLA Ops:
  0.0 14.0 %copy-start = (s32[8,5]{1,0:T(8,128)S(1)}, s32[8,5]{1,0:T(8,128)}, u32[]{:S(2)}) copy-start(s32[8,5]{1,0:T(8,128)} %param.3) | copy-start | bytes 484
  0.0 21.5 %all-to-all-start = ((f32[8,5,16,128]{3,2,1,0:T(8,128)}), f32[8,5,16,128]{3,2,1,0:T(8,128)S(1)}, u32[]{:S(2)}, u32[]{:S(2)}) async-start(f32[8,5,16,128]{3,2,1,0:T(8,128)} %param.2), calls=%async_computation | async-start | bytes 655360 | tf_op jit(solution)/shard_map/all_to_all | solution.py:107
  21.7 8.0 %collective-permute-start = (f32[4,128,128]{2,1,0:T(8,128)S(1)}, f32[4,128,128]{2,1,0:T(8,128)S(1)}, u32[]{:S(2)}, u32[]{:S(2)}) collective-permute-start(f32[4,128,128]{2,1,0:T(8,128)S(1)} %get-tuple-element.9), channel_id=1, source_target_pairs={{16,20},{20,16},{24,28},{28,24},{0,4},{4,0},{8,12},{12,8},{13,9},{... | collective-permute-start | bytes 786440 | tf_op jit(solution)/shard_map/ppermute | solution.py:117
  23.6 10.1 %collective-permute-start.1 = (f32[4,128,128]{2,1,0:T(8,128)S(1)}, f32[4,128,128]{2,1,0:T(8,128)S(1)}, u32[]{:S(2)}, u32[]{:S(2)}) collective-permute-start(f32[4,128,128]{2,1,0:T(8,128)S(1)} %get-tuple-element.10), channel_id=1, source_target_pairs={{20,24},{24,20},{28,0},{0,28},{4,8},{8,4},{12,13},{13,12},{9,5},{5... | collective-permute-start | bytes 786440 | tf_op jit(solution)/shard_map/ppermute | solution.py:116
  29.7 7.8 %collective-permute-start.2 = (f32[3,128,128]{2,1,0:T(8,128)S(1)}, f32[3,128,128]{2,1,0:T(8,128)S(1)}, u32[]{:S(2)}, u32[]{:S(2)}) collective-permute-start(f32[3,128,128]{2,1,0:T(8,128)S(1)} %constant_dynamic-slice_fusion.1), channel_id=1, source_target_pairs={{20,24},{24,20},{28,0},{0,28},{4,8},{8,4},{12,13},{13,12},{9,5},{5... | collective-permute-start | bytes 589832 | tf_op jit(solution)/shard_map/ppermute | solution.py:118
  33.7 6.7 %collective-permute-start.3 = (f32[3,128,128]{2,1,0:T(8,128)S(1)}, f32[3,128,128]{2,1,0:T(8,128)S(1)}, u32[]{:S(2)}, u32[]{:S(2)}) collective-permute-start(f32[3,128,128]{2,1,0:T(8,128)S(1)} %constant_dynamic-slice_fusion), channel_id=1, source_target_pairs={{16,20},{20,16},{24,28},{28,24},{0,4},{4,0},{8,12},{12,8},{13,9},{... | collective-permute-start | bytes 589832 | tf_op jit(solution)/shard_map/ppermute | solution.py:119

commit v5 on v4

--- a/solution.py
+++ b/solution.py
@@ -37,6 +37,15 @@
     return flip, ((lax.axis_index("col") + cols - START) % cols) ^ flip
 
 
+def return_groups(sizes):
+    rows, cols, depths = sizes
+    return [
+        [(row * cols + (START + j) % cols) * depths + depth for j in range(cols)]
+        for row in range(rows)
+        for depth in range(depths)
+    ]
+
+
 def halves(value):
     high = value.astype(jnp.bfloat16)
     return high, (value - high.astype(jnp.float32)).astype(jnp.bfloat16)
@@ -61,7 +70,7 @@
 
 def band_kernel(marks_ref, own_ref, near_ref, far_ref, relayed_ref, handed_ref, out_ref):
     parts, _, rows, _ = out_ref.shape
-    flip, row = place()
+    _, row = place()
     even = row & 1 == 0
     right = {(HALF, s): halves(own_ref[s]) for s in range(WIDE)}
     for s in range(WIDE - 1):
@@ -91,7 +100,18 @@
     for t in range(WIDE):
         value = 3.0 * square[t] - 2.0 * cube[t]
         for part in range(parts):
-            out_ref[(part - START) % parts ^ flip, t] = value[part * rows : (part + 1) * rows]
+            out_ref[(part - START) % parts, t] = value[part * rows : (part + 1) * rows]
+
+
+def order_kernel(back_ref, out_ref, sems):
+    flip, _ = place()
+    copies = [
+        pltpu.make_async_copy(back_ref.at[r ^ flip], out_ref.at[r], sems.at[r]) for r in range(out_ref.shape[0])
+    ]
+    for copy in copies:
+        copy.start()
+    for copy in copies:
+        copy.wait()
 
 
 def shards(density, pattern):
@@ -124,7 +144,15 @@
         out_specs=VMEM,
         compiler_params=PARAMS,
     )(marks, own, near, far, relayed, handed)
-    return lax.all_to_all(result, AXES, 0, 0, axis_index_groups=groups, tiled=True)
+    back = lax.all_to_all(result, AXES, 0, 0, axis_index_groups=return_groups(sizes), tiled=True)
+    return pl.pallas_call(
+        order_kernel,
+        out_shape=jax.ShapeDtypeStruct(density.shape, jnp.float32),
+        in_specs=[VMEM],
+        out_specs=pl.BlockSpec(memory_space=pl.ANY),
+        scratch_shapes=[pltpu.SemaphoreType.DMA((cols,))],
+        compiler_params=PARAMS,
+    )(back)
 
 
 def solution(mesh):

time: 62.6 us -> 62.3 us (level)
  Pallas kernels: 1.36 us -> 2.14 us
  local copies, waits for them, and re-layouts: 0.77 us -> 0.04 us
    pallas_call x0 -> x1, Pallas kernels: none -> 0.78 us  [shards(): pl.pallas_call(order_kernel, out_shape=jax.ShapeDtypeStruct(density.shape...]
    unnamed x3 -> x2, local copies, waits for them, and re-layouts: 0.73 us -> 0.01 us
where the time goes in v5:
time: 62.3 us; the launch traced here: 61.5 us
  starting transfers between devices  27.1 us (43%)
  blocking collectives  19.1 us (31%)
  waiting for transfers between devices  13 us (21%)
  Pallas kernels  2.14 us (3%)
    all_to_all x1, blocking collectives, shards(): lax.all_to_all(result, AXES, 0, 0, axis_index_groups=return_groups(sizes)...  19.1 us
    all_to_all x1, starting transfers between devices, shards(): lax.all_to_all(density, AXES, 0, 0, axis_index_groups=groups, tiled=True)  14 us
    all_to_all x1, waiting for transfers between devices, shards(): lax.all_to_all(density, AXES, 0, 0, axis_index_groups=groups, tiled=True)  7.49 us
    ppermute x1, starting transfers between devices, shards(): far = lax.ppermute(far, AXES, outside)  4.47 us
    ppermute x1, starting transfers between devices, shards(): lax.ppermute(lax.dynamic_slice_in_dim(near, odd, wide - 2, 0), AXES, outs...  3.97 us
    ppermute x1, waiting for transfers between devices, shards(): lax.ppermute(lax.dynamic_slice_in_dim(far, 1 - odd, wide - 2, 0), AXES, i...  2.87 us
    ppermute x1, starting transfers between devices, shards(): lax.ppermute(lax.dynamic_slice_in_dim(far, 1 - odd, wide - 2, 0), AXES, i...  2.82 us
    ppermute x1, starting transfers between devices, shards(): near = lax.ppermute(near, AXES, inside)  1.92 us
  transfers between devices with their start and end apart: 5, of which 4 were waited for; matrix products, arithmetic and copies ran while one was open for 0% of the time, Pallas kernels for 0%

profile of v5, /device:TPU:1, one launch (start us, length us, event | category | flops | bytes accessed | tf_op | source)
XLA Modules:
  0.0 61.5 jit_solution(8393520903588257133)
XLA Ops:
  0.0 0.0 copy-start
  0.0 14.0 %all-to-all-start = ((f32[8,5,16,128]{3,2,1,0:T(8,128)}), f32[8,5,16,128]{3,2,1,0:T(8,128)S(1)}, u32[]{:S(2)}, u32[]{:S(2)}) async-start(f32[8,5,16,128]{3,2,1,0:T(8,128)} %param.2), calls=%async_computation | async-start | bytes 655360 | tf_op jit(solution)/shard_map/all_to_all | solution.py:127
  14.0 0.0 copy-done
  14.0 7.5 %all-to-all-done.parts_ref = f32[8,5,16,128]{3,2,1,0:T(8,128)S(1)} async-done(((f32[8,5,16,128]{3,2,1,0:T(8,128)}), f32[8,5,16,128]{3,2,1,0:T(8,128)S(1)}, u32[]{:S(2)}, u32[]{:S(2)}) %all-to-all-start) | async-done | bytes 327712 | tf_op jit(solution)/shard_map/all_to_all | solution.py:127
  21.5 0.2 shard_map.28
  21.7 1.9 %collective-permute-start = (f32[4,128,128]{2,1,0:T(8,128)S(1)}, f32[4,128,128]{2,1,0:T(8,128)S(1)}, u32[]{:S(2)}, u32[]{:S(2)}) collective-permute-start(f32[4,128,128]{2,1,0:T(8,128)S(1)} %get-tuple-element.9), channel_id=1, source_target_pairs={{16,20},{20,16},{24,28},{28,24},{0,4},{4,0},{8,12},{12,8},{13,9},{... | collective-permute-start | bytes 786440 | tf_op jit(solution)/shard_map/ppermute | solution.py:137
  23.6 4.5 %collective-permute-start.1 = (f32[4,128,128]{2,1,0:T(8,128)S(1)}, f32[4,128,128]{2,1,0:T(8,128)S(1)}, u32[]{:S(2)}, u32[]{:S(2)}) collective-permute-start(f32[4,128,128]{2,1,0:T(8,128)S(1)} %get-tuple-element.10), channel_id=1, source_target_pairs={{20,24},{24,20},{28,0},{0,28},{4,8},{8,4},{12,13},{13,12},{9,5},{5... | collective-permute-start | bytes 786440 | tf_op jit(solution)/shard_map/ppermute | solution.py:136
  28.1 1.6 %collective-permute-done.near_ref = f32[4,128,128]{2,1,0:T(8,128)S(1)} collective-permute-done((f32[4,128,128]{2,1,0:T(8,128)S(1)}, f32[4,128,128]{2,1,0:T(8,128)S(1)}, u32[]{:S(2)}, u32[]{:S(2)}) %collective-permute-start) | collective-permute-done | bytes 262176 | tf_op jit(solution)/shard_map/ppermute | solution.py:137
  29.7 4.0 %collective-permute-start.2 = (f32[3,128,128]{2,1,0:T(8,128)S(1)}, f32[3,128,128]{2,1,0:T(8,128)S(1)}, u32[]{:S(2)}, u32[]{:S(2)}) collective-permute-start(f32[3,128,128]{2,1,0:T(8,128)S(1)} %constant_dynamic-slice_fusion.1), channel_id=1, source_target_pairs={{20,24},{24,20},{28,0},{0,28},{4,8},{8,4},{12,13},{13,12},{9,5},{5... | collective-permute-start | bytes 589832 | tf_op jit(solution)/shard_map/ppermute | solution.py:138
  33.7 0.0 collective-permute-done.1.far_ref
  33.7 2.8 %collective-permute-start.3 = (f32[3,128,128]{2,1,0:T(8,128)S(1)}, f32[3,128,128]{2,1,0:T(8,128)S(1)}, u32[]{:S(2)}, u32[]{:S(2)}) collective-permute-start(f32[3,128,128]{2,1,0:T(8,128)S(1)} %constant_dynamic-slice_fusion), channel_id=1, source_target_pairs={{16,20},{20,16},{24,28},{28,24},{0,4},{4,0},{8,12},{12,8},{13,9},{... | collective-permute-start | bytes 589832 | tf_op jit(solution)/shard_map/ppermute | solution.py:139
  36.6 1.0 %collective-permute-done.2.relayed_ref = f32[3,128,128]{2,1,0:T(8,128)S(1)} collective-permute-done((f32[3,128,128]{2,1,0:T(8,128)S(1)}, f32[3,128,128]{2,1,0:T(8,128)S(1)}, u32[]{:S(2)}, u32[]{:S(2)}) %collective-permute-start.2) | collective-permute-done | bytes 196640 | tf_op jit(solution)/shard_map/ppermute | solution.py:138
  37.6 2.9 %collective-permute-done.3.handed_ref = f32[3,128,128]{2,1,0:T(8,128)S(1)} collective-permute-done((f32[3,128,128]{2,1,0:T(8,128)S(1)}, f32[3,128,128]{2,1,0:T(8,128)S(1)}, u32[]{:S(2)}, u32[]{:S(2)}) %collective-permute-start.3) | collective-permute-done | bytes 196640 | tf_op jit(solution)/shard_map/ppermute | solution.py:139
  40.4 1.2 %shard_map.29 = f32[8,5,16,128]{3,2,1,0:T(8,128)S(1)} custom-call(f32[8,128]{1,0:T(8,128)S(1)} %pad.4.marks_ref, f32[5,128,128]{2,1,0:T(8,128)S(1)} %get-tuple-element.8.own_ref, f32[4,128,128]{2,1,0:T(8,128)S(1)} %collective-permute-done.near_ref, f32[4,128,128]{2,1,0:T(8,128)S(1)} %collective-permute-done.1.far_ref, ...), custom_call_target="tpu_custom_call" | custom-call | tf_op jit(solution)/shard_map/pallas_call | solution.py:140
  41.6 19.1 %all_to_all.10.back_ref = f32[8,5,16,128]{3,2,1,0:T(8,128)S(1)} all-to-all(f32[8,5,16,128]{3,2,1,0:T(8,128)S(1)} %shard_map.29), channel_id=1, replica_groups={{16,20,24,28,0,4,8,12},{17,21,25,29,1,5,9,13},{18,22,26,30,2,6,10,14},{..., dimensions={0} | all-to-all | bytes 655360 | tf_op jit(solution)/shard_map/all_to_all | solution.py:147
  60.7 0.8 %shard_map.30 = f32[8,5,16,128]{3,2,1,0:T(8,128)} custom-call(f32[8,5,16,128]{3,2,1,0:T(8,128)S(1)} %all_to_all.10.back_ref), custom_call_target="tpu_custom_call" | custom-call | tf_op jit(solution)/shard_map/pallas_call | solution.py:148
  (4 shorter events, 0.0 us)
Async XLA Ops:
  0.0 14.0 %copy-start = (s32[8,5]{1,0:T(8,128)S(1)}, s32[8,5]{1,0:T(8,128)}, u32[]{:S(2)}) copy-start(s32[8,5]{1,0:T(8,128)} %param.3) | copy-start | bytes 484
  0.0 21.5 %all-to-all-start = ((f32[8,5,16,128]{3,2,1,0:T(8,128)}), f32[8,5,16,128]{3,2,1,0:T(8,128)S(1)}, u32[]{:S(2)}, u32[]{:S(2)}) async-start(f32[8,5,16,128]{3,2,1,0:T(8,128)} %param.2), calls=%async_computation | async-start | bytes 655360 | tf_op jit(solution)/shard_map/all_to_all | solution.py:127
  21.7 8.0 %collective-permute-start = (f32[4,128,128]{2,1,0:T(8,128)S(1)}, f32[4,128,128]{2,1,0:T(8,128)S(1)}, u32[]{:S(2)}, u32[]{:S(2)}) collective-permute-start(f32[4,128,128]{2,1,0:T(8,128)S(1)} %get-tuple-element.9), channel_id=1, source_target_pairs={{16,20},{20,16},{24,28},{28,24},{0,4},{4,0},{8,12},{12,8},{13,9},{... | collective-permute-start | bytes 786440 | tf_op jit(solution)/shard_map/ppermute | solution.py:137
  23.6 10.1 %collective-permute-start.1 = (f32[4,128,128]{2,1,0:T(8,128)S(1)}, f32[4,128,128]{2,1,0:T(8,128)S(1)}, u32[]{:S(2)}, u32[]{:S(2)}) collective-permute-start(f32[4,128,128]{2,1,0:T(8,128)S(1)} %get-tuple-element.10), channel_id=1, source_target_pairs={{20,24},{24,20},{28,0},{0,28},{4,8},{8,4},{12,13},{13,12},{9,5},{5... | collective-permute-start | bytes 786440 | tf_op jit(solution)/shard_map/ppermute | solution.py:136
  29.7 7.8 %collective-permute-start.2 = (f32[3,128,128]{2,1,0:T(8,128)S(1)}, f32[3,128,128]{2,1,0:T(8,128)S(1)}, u32[]{:S(2)}, u32[]{:S(2)}) collective-permute-start(f32[3,128,128]{2,1,0:T(8,128)S(1)} %constant_dynamic-slice_fusion.1), channel_id=1, source_target_pairs={{20,24},{24,20},{28,0},{0,28},{4,8},{8,4},{12,13},{13,12},{9,5},{5... | collective-permute-start | bytes 589832 | tf_op jit(solution)/shard_map/ppermute | solution.py:138
  33.7 6.7 %collective-permute-start.3 = (f32[3,128,128]{2,1,0:T(8,128)S(1)}, f32[3,128,128]{2,1,0:T(8,128)S(1)}, u32[]{:S(2)}, u32[]{:S(2)}) collective-permute-start(f32[3,128,128]{2,1,0:T(8,128)S(1)} %constant_dynamic-slice_fusion), channel_id=1, source_target_pairs={{16,20},{20,16},{24,28},{28,24},{0,4},{4,0},{8,12},{12,8},{13,9},{... | collective-permute-start | bytes 589832 | tf_op jit(solution)/shard_map/ppermute | solution.py:139

commit v6 on v4

--- a/solution.py
+++ b/solution.py
@@ -9,7 +9,6 @@
 WIDE = 5
 AXES = ("row", "col", "depth")
 START = 4
-TURNED = 1
 VMEM = pl.BlockSpec(memory_space=pltpu.VMEM)
 PARAMS = pltpu.CompilerParams(vmem_limit_bytes=32 * 1024 * 1024)
 
@@ -18,8 +17,7 @@
     rows, cols, depths = sizes
     chunk, at = divmod(i % (rows * cols * depths), cols)
     row, depth = divmod(chunk, depths)
-    col = (START + (cols - 1 - at if chunk % 2 == TURNED else at)) % cols
-    return (row * cols + col) * depths + depth
+    return (row * cols + (START + at) % cols) * depths + depth
 
 
 def exchange(sizes, first):
@@ -30,11 +28,9 @@
     return result
 
 
-def place():
+def own_row():
     cols = lax.axis_size("col")
-    chunk = lax.axis_index("row") * lax.axis_size("depth") + lax.axis_index("depth")
-    flip = jnp.where((chunk & 1) == TURNED, cols - 1, 0)
-    return flip, ((lax.axis_index("col") + cols - START) % cols) ^ flip
+    return (lax.axis_index("col") + cols - START) % cols
 
 
 def halves(value):
@@ -48,12 +44,12 @@
 
 def arrange_kernel(marks_ref, parts_ref, own_ref, near_ref, far_ref):
     parts, _, rows, _ = parts_ref.shape
-    flip, row = place()
+    row = own_row()
     odd = row & 1
     for slot in range(WIDE):
         keep = marks_ref[pl.ds(row, 1), slot : slot + 1]
         for part in range(parts):
-            own_ref[slot, part * rows : (part + 1) * rows] = parts_ref[(part - START) % parts ^ flip, slot] * keep
+            own_ref[slot, part * rows : (part + 1) * rows] = parts_ref[(part - START) % parts, slot] * keep
     for slot in range(WIDE - 1):
         near_ref[slot] = own_ref[slot + 1 - odd]
         far_ref[slot] = own_ref[slot + odd]
@@ -61,7 +57,7 @@
 
 def band_kernel(marks_ref, own_ref, near_ref, far_ref, relayed_ref, handed_ref, out_ref):
     parts, _, rows, _ = out_ref.shape
-    flip, row = place()
+    row = own_row()
     even = row & 1 == 0
     right = {(HALF, s): halves(own_ref[s]) for s in range(WIDE)}
     for s in range(WIDE - 1):
@@ -91,7 +87,7 @@
     for t in range(WIDE):
         value = 3.0 * square[t] - 2.0 * cube[t]
         for part in range(parts):
-            out_ref[(part - START) % parts ^ flip, t] = value[part * rows : (part + 1) * rows]
+            out_ref[(part - START) % parts, t] = value[part * rows : (part + 1) * rows]
 
 
 def shards(density, pattern):
@@ -99,7 +95,7 @@
     cols, wide, rows, width = density.shape
     groups = [[owner(sizes, i + j) for j in range(cols)] for i in range(0, sizes[0] * sizes[1] * sizes[2], cols)]
     inside, outside = exchange(sizes, 0), exchange(sizes, 1)
-    odd = place()[1] & 1
+    odd = own_row() & 1
 
     def blocks(n):
         return jax.ShapeDtypeStruct((n, cols * rows, width), jnp.float32)

time: 62.6 us -> 61.3 us (0.979)
  the two profiles are of different devices: /device:TPU:1 before, /device:TPU:30 now
where the time goes in v6:
time: 61.3 us; the launch traced here: 60.9 us
  starting transfers between devices  27.8 us (45%)
  blocking collectives  16.3 us (27%)
  waiting for transfers between devices  14.5 us (24%)
  Pallas kernels  1.37 us (2%)
  local copies, waits for them, and re-layouts  0.77 us (1%)
    all_to_all x1, blocking collectives, shards(): lax.all_to_all(result, AXES, 0, 0, axis_index_groups=groups, tiled=True)  16.3 us
    all_to_all x1, starting transfers between devices, shards(): lax.all_to_all(density, AXES, 0, 0, axis_index_groups=groups, tiled=True)  13.7 us
    all_to_all x1, waiting for transfers between devices, shards(): lax.all_to_all(density, AXES, 0, 0, axis_index_groups=groups, tiled=True)  7.89 us
    ppermute x1, starting transfers between devices, shards(): lax.ppermute(lax.dynamic_slice_in_dim(near, odd, wide - 2, 0), AXES, outs...  4.25 us
    ppermute x1, starting transfers between devices, shards(): far = lax.ppermute(far, AXES, outside)  3.8 us
    ppermute x1, starting transfers between devices, shards(): near = lax.ppermute(near, AXES, inside)  3.37 us
    ppermute x1, waiting for transfers between devices, shards(): lax.ppermute(lax.dynamic_slice_in_dim(far, 1 - odd, wide - 2, 0), AXES, i...  3.08 us
    ppermute x1, starting transfers between devices, shards(): lax.ppermute(lax.dynamic_slice_in_dim(far, 1 - odd, wide - 2, 0), AXES, i...  2.68 us
  transfers between devices with their start and end apart: 5, of which 4 were waited for; matrix products, arithmetic and copies ran while one was open for 0% of the time, Pallas kernels for 0%

profile of v6, /device:TPU:30, one launch (start us, length us, event | category | flops | bytes accessed | tf_op | source)
XLA Modules:
  0.0 60.9 jit_solution(9381348163391210398)
XLA Ops:
  0.0 0.0 copy-start
  0.0 13.7 %all-to-all-start = ((f32[8,5,16,128]{3,2,1,0:T(8,128)}), f32[8,5,16,128]{3,2,1,0:T(8,128)S(1)}, u32[]{:S(2)}, u32[]{:S(2)}) async-start(f32[8,5,16,128]{3,2,1,0:T(8,128)} %param.2), calls=%async_computation | async-start | bytes 655360 | tf_op jit(solution)/shard_map/all_to_all | solution.py:103
  13.7 0.0 copy-done
  13.7 7.9 %all-to-all-done.parts_ref = f32[8,5,16,128]{3,2,1,0:T(8,128)S(1)} async-done(((f32[8,5,16,128]{3,2,1,0:T(8,128)}), f32[8,5,16,128]{3,2,1,0:T(8,128)S(1)}, u32[]{:S(2)}, u32[]{:S(2)}) %all-to-all-start) | async-done | bytes 327712 | tf_op jit(solution)/shard_map/all_to_all | solution.py:103
  21.6 0.2 shard_map.28
  21.8 3.4 %collective-permute-start = (f32[4,128,128]{2,1,0:T(8,128)S(1)}, f32[4,128,128]{2,1,0:T(8,128)S(1)}, u32[]{:S(2)}, u32[]{:S(2)}) collective-permute-start(f32[4,128,128]{2,1,0:T(8,128)S(1)} %get-tuple-element.9), channel_id=1, source_target_pairs={{16,20},{20,16},{24,28},{28,24},{0,4},{4,0},{8,12},{12,8},{17,21},... | collective-permute-start | bytes 786440 | tf_op jit(solution)/shard_map/ppermute | solution.py:113
  25.2 3.8 %collective-permute-start.1 = (f32[4,128,128]{2,1,0:T(8,128)S(1)}, f32[4,128,128]{2,1,0:T(8,128)S(1)}, u32[]{:S(2)}, u32[]{:S(2)}) collective-permute-start(f32[4,128,128]{2,1,0:T(8,128)S(1)} %get-tuple-element.10), channel_id=1, source_target_pairs={{20,24},{24,20},{28,0},{0,28},{4,8},{8,4},{12,17},{17,12},{21,25},... | collective-permute-start | bytes 786440 | tf_op jit(solution)/shard_map/ppermute | solution.py:112
  29.0 1.8 %collective-permute-done.near_ref = f32[4,128,128]{2,1,0:T(8,128)S(1)} collective-permute-done((f32[4,128,128]{2,1,0:T(8,128)S(1)}, f32[4,128,128]{2,1,0:T(8,128)S(1)}, u32[]{:S(2)}, u32[]{:S(2)}) %collective-permute-start) | collective-permute-done | bytes 262176 | tf_op jit(solution)/shard_map/ppermute | solution.py:113
  30.8 4.2 %collective-permute-start.2 = (f32[3,128,128]{2,1,0:T(8,128)S(1)}, f32[3,128,128]{2,1,0:T(8,128)S(1)}, u32[]{:S(2)}, u32[]{:S(2)}) collective-permute-start(f32[3,128,128]{2,1,0:T(8,128)S(1)} %constant_dynamic-slice_fusion.1), channel_id=1, source_target_pairs={{20,24},{24,20},{28,0},{0,28},{4,8},{8,4},{12,17},{17,12},{21,25},... | collective-permute-start | bytes 589832 | tf_op jit(solution)/shard_map/ppermute | solution.py:114
  35.0 0.0 collective-permute-done.1.far_ref
  35.1 2.7 %collective-permute-start.3 = (f32[3,128,128]{2,1,0:T(8,128)S(1)}, f32[3,128,128]{2,1,0:T(8,128)S(1)}, u32[]{:S(2)}, u32[]{:S(2)}) collective-permute-start(f32[3,128,128]{2,1,0:T(8,128)S(1)} %constant_dynamic-slice_fusion), channel_id=1, source_target_pairs={{16,20},{20,16},{24,28},{28,24},{0,4},{4,0},{8,12},{12,8},{17,21},... | collective-permute-start | bytes 589832 | tf_op jit(solution)/shard_map/ppermute | solution.py:115
  37.8 1.8 %collective-permute-done.2.relayed_ref = f32[3,128,128]{2,1,0:T(8,128)S(1)} collective-permute-done((f32[3,128,128]{2,1,0:T(8,128)S(1)}, f32[3,128,128]{2,1,0:T(8,128)S(1)}, u32[]{:S(2)}, u32[]{:S(2)}) %collective-permute-start.2) | collective-permute-done | bytes 196640 | tf_op jit(solution)/shard_map/ppermute | solution.py:114
  39.6 3.1 %collective-permute-done.3.handed_ref = f32[3,128,128]{2,1,0:T(8,128)S(1)} collective-permute-done((f32[3,128,128]{2,1,0:T(8,128)S(1)}, f32[3,128,128]{2,1,0:T(8,128)S(1)}, u32[]{:S(2)}, u32[]{:S(2)}) %collective-permute-start.3) | collective-permute-done | bytes 196640 | tf_op jit(solution)/shard_map/ppermute | solution.py:115
  42.6 1.2 %shard_map.29 = f32[8,5,16,128]{3,2,1,0:T(8,128)S(1)} custom-call(f32[8,128]{1,0:T(8,128)S(1)} %pad.4.marks_ref, f32[5,128,128]{2,1,0:T(8,128)S(1)} %get-tuple-element.8.own_ref, f32[4,128,128]{2,1,0:T(8,128)S(1)} %collective-permute-done.near_ref, f32[4,128,128]{2,1,0:T(8,128)S(1)} %collective-permute-done.1.far_ref, ...), custom_call_target="tpu_custom_call" | custom-call | tf_op jit(solution)/shard_map/pallas_call | solution.py:116
  43.9 16.3 %all_to_all.10 = f32[8,5,16,128]{3,2,1,0:T(8,128)S(1)} all-to-all(f32[8,5,16,128]{3,2,1,0:T(8,128)S(1)} %shard_map.29), channel_id=1, replica_groups={{16,20,24,28,0,4,8,12},{17,21,25,29,1,5,9,13},{18,22,26,30,2,6,10,14},{..., dimensions={0} | all-to-all | bytes 655360 | tf_op jit(solution)/shard_map/all_to_all | solution.py:123
  60.2 0.7 %copy.4 = f32[8,5,16,128]{3,2,1,0:T(8,128)} copy(f32[8,5,16,128]{3,2,1,0:T(8,128)S(1)} %all_to_all.10) | data formatting | bytes 655360
  (4 shorter events, 0.0 us)
Async XLA Ops:
  0.0 13.7 %copy-start = (s32[8,5]{1,0:T(8,128)S(1)}, s32[8,5]{1,0:T(8,128)}, u32[]{:S(2)}) copy-start(s32[8,5]{1,0:T(8,128)} %param.3) | copy-start | bytes 484
  0.0 21.6 %all-to-all-start = ((f32[8,5,16,128]{3,2,1,0:T(8,128)}), f32[8,5,16,128]{3,2,1,0:T(8,128)S(1)}, u32[]{:S(2)}, u32[]{:S(2)}) async-start(f32[8,5,16,128]{3,2,1,0:T(8,128)} %param.2), calls=%async_computation | async-start | bytes 655360 | tf_op jit(solution)/shard_map/all_to_all | solution.py:103
  21.8 9.0 %collective-permute-start = (f32[4,128,128]{2,1,0:T(8,128)S(1)}, f32[4,128,128]{2,1,0:T(8,128)S(1)}, u32[]{:S(2)}, u32[]{:S(2)}) collective-permute-start(f32[4,128,128]{2,1,0:T(8,128)S(1)} %get-tuple-element.9), channel_id=1, source_target_pairs={{16,20},{20,16},{24,28},{28,24},{0,4},{4,0},{8,12},{12,8},{17,21},... | collective-permute-start | bytes 786440 | tf_op jit(solution)/shard_map/ppermute | solution.py:113
  25.2 9.9 %collective-permute-start.1 = (f32[4,128,128]{2,1,0:T(8,128)S(1)}, f32[4,128,128]{2,1,0:T(8,128)S(1)}, u32[]{:S(2)}, u32[]{:S(2)}) collective-permute-start(f32[4,128,128]{2,1,0:T(8,128)S(1)} %get-tuple-element.10), channel_id=1, source_target_pairs={{20,24},{24,20},{28,0},{0,28},{4,8},{8,4},{12,17},{17,12},{21,25},... | collective-permute-start | bytes 786440 | tf_op jit(solution)/shard_map/ppermute | solution.py:112
  30.8 8.8 %collective-permute-start.2 = (f32[3,128,128]{2,1,0:T(8,128)S(1)}, f32[3,128,128]{2,1,0:T(8,128)S(1)}, u32[]{:S(2)}, u32[]{:S(2)}) collective-permute-start(f32[3,128,128]{2,1,0:T(8,128)S(1)} %constant_dynamic-slice_fusion.1), channel_id=1, source_target_pairs={{20,24},{24,20},{28,0},{0,28},{4,8},{8,4},{12,17},{17,12},{21,25},... | collective-permute-start | bytes 589832 | tf_op jit(solution)/shard_map/ppermute | solution.py:114
  35.1 7.6 %collective-permute-start.3 = (f32[3,128,128]{2,1,0:T(8,128)S(1)}, f32[3,128,128]{2,1,0:T(8,128)S(1)}, u32[]{:S(2)}, u32[]{:S(2)}) collective-permute-start(f32[3,128,128]{2,1,0:T(8,128)S(1)} %constant_dynamic-slice_fusion), channel_id=1, source_target_pairs={{16,20},{20,16},{24,28},{28,24},{0,4},{4,0},{8,12},{12,8},{17,21},... | collective-permute-start | bytes 589832 | tf_op jit(solution)/shard_map/ppermute | solution.py:115
